TPU v7x, 128 devices: a whole 4x4x4 slice. The times are simulated.
128 devices in a mesh: gx: 8 (over x, core), gy: 16 (over y, z).
Axes of the slice: x: 4, y: 4, z: 4, core: 2. Of those that a mesh axis runs over, the one named last changes fastest.
Arguments:
- right_side: float32 [256, 512, 512], P('gx', 'gy'), may hold values from -120 to 120
- absorption: float32 [256, 512, 512], P('gx', 'gy'), may hold values from 0.001 to 0.05
Outputs:
- solution: float32 [256, 512, 512], P('gx', 'gy')
All inputs are finite; a program needn't handle non-finite values.
Results may differ from a plain program's by a relative error of at most 0.00002.
Values sent between devices are 32-bit elements; how exact they have to be, the bound alone decides.
A program may use at most 128 MiB of HBM per device.

v0:
```python
from functools import partial

import jax
import jax.numpy as jnp
from jax import lax
from jax.sharding import PartitionSpec as P

LEVELS = 6
DEGREE = 4


center_value = 0.7875
half_width = 0.6125
agglomerate_level = 3


def padded_2(value, sides, width):
    for axis, dim in sides:
        peers, length = (lax.axis_size(axis), value.shape[dim])
        up = [(i, (i + 1) % peers) for i in range(peers - 1)]
        down = [(j, i) for i, j in up]
        last = lax.slice_in_dim(value, length - width, length, axis=dim)
        first = lax.slice_in_dim(value, 0, width, axis=dim)
        before = lax.ppermute(last, axis, up)
        after = lax.ppermute(first, axis, down)
        value = jnp.concatenate([before, value, after], axis=dim)
    return value


def from_behind(block, axis, distance):
    devices = range(lax.axis_size(axis))
    route = [(i - distance, i) for i in devices if i - distance in devices]
    return lax.ppermute(block, axis, route)


def box_total(padded):
    along_x = padded[:-2] + padded[1:-1] + padded[2:]
    along_y = along_x[:, :-2] + along_x[:, 1:-1] + along_x[:, 2:]
    return along_y[:, :, :-2] + along_y[:, :, 1:-1] + along_y[:, :, 2:]


def fine_pad(field):
    return padded_2(field, (("gx", 0), ("gy", 1)), 1)


def slab_pad(field):
    padded = padded_2(field, (("gx", 0),), 1)
    return jnp.pad(padded, ((0, 0), (1, 1), (0, 0)))


def apply_op(field, diagonal, padder):
    padded = jnp.pad(padder(field), ((0, 0), (0, 0), (1, 1)))
    return (diagonal + 1.0) * field - box_total(padded)


def chebyshev(start, source, diagonal, operate):
    if start is None:
        residue = source / diagonal
    else:
        residue = (source - operate(start)) / diagonal
    update = residue / center_value
    ratio = half_width / center_value
    field = start
    for iteration in range(DEGREE):
        field = update if field is None else field + update
        if iteration < DEGREE - 1:
            residue = residue - operate(update) / diagonal
            ratio_next = 1.0 / (2.0 * center_value / half_width - ratio)
            update = ratio_next * ratio * update + 2.0 * ratio_next / half_width * residue
            ratio = ratio_next
    return field


def restrict_dim(field, dim, border):
    count = field.shape[dim]
    joined = jnp.concatenate([field, border], axis=dim)
    first = lax.slice_in_dim(joined, 0, count, 2, dim)
    middle = lax.slice_in_dim(joined, 1, count, 2, dim)
    last = lax.slice_in_dim(joined, 2, count + 1, 2, dim)
    return 0.25 * first + 0.5 * middle + 0.25 * last


def prolong_dim(coarse, dim, border):
    count = coarse.shape[dim]
    joined = jnp.concatenate([border, coarse], axis=dim)
    before = lax.slice_in_dim(joined, 0, count, 1, dim)
    even_part = 0.5 * (before + coarse)
    stacked = jnp.stack([even_part, coarse], axis=dim + 1)
    new_shape = list(coarse.shape)
    new_shape[dim] = 2 * count
    return stacked.reshape(new_shape)


def restrict_pair(residue, absorption, remote_y):
    border = jnp.stack([residue[0:1], absorption[0:1]])
    border = from_behind(border, "gx", -1)
    residue = restrict_dim(residue, 0, border[0])
    absorption = restrict_dim(absorption, 0, border[1])
    border = jnp.stack([residue[:, 0:1], absorption[:, 0:1]])
    if remote_y:
        border = from_behind(border, "gy", -1)
    else:
        border = jnp.zeros_like(border)
    residue = restrict_dim(residue, 1, border[0])
    absorption = restrict_dim(absorption, 1, border[1])
    residue = restrict_dim(residue, 2, jnp.zeros_like(residue[:, :, 0:1]))
    absorption = restrict_dim(absorption, 2, jnp.zeros_like(absorption[:, :, 0:1]))
    return (residue, absorption)


def prolong_field(coarse, remote_y):
    border = coarse[-1:]
    border = from_behind(border, "gx", 1)
    finer = prolong_dim(coarse, 0, border)
    border = finer[:, -1:]
    if remote_y:
        border = from_behind(border, "gy", 1)
    else:
        border = jnp.zeros_like(border)
    finer = prolong_dim(finer, 1, border)
    return prolong_dim(finer, 2, jnp.zeros_like(finer[:, :, -1:]))


def coarse_cycle(depth_level, source, absorption, padder, remote_x):
    diagonal = 26.0 + absorption
    operate = partial(apply_op, diagonal=diagonal, padder=padder)
    field = chebyshev(None, source, diagonal, operate)
    if depth_level < LEVELS - 1:
        residue = source - operate(field)
        coarse_source, coarse_absorb = restrict_pair(residue, absorption, False)
        correction = coarse_cycle(
            depth_level + 1, 4.0 * coarse_source, 4.0 * coarse_absorb, padder, remote_x
        )
        field = field + prolong_field(correction, False)
    return chebyshev(field, source, diagonal, operate)


def agglomerate(source, absorption):
    rows, columns, layers = source.shape
    all_source, all_absorb = (
        lax.all_gather(source, "gy", axis=1, tiled=True),
        lax.all_gather(absorption, "gy", axis=1, tiled=True),
    )
    correction = coarse_cycle(agglomerate_level, all_source, all_absorb, slab_pad, True)
    return lax.dynamic_slice_in_dim(correction, lax.axis_index("gy") * columns, columns, 1)


def fine_cycle(depth_level, source, absorption):
    diagonal = 26.0 + absorption
    operate = partial(apply_op, diagonal=diagonal, padder=fine_pad)
    field = chebyshev(None, source, diagonal, operate)
    residue = source - operate(field)
    coarse_source, coarse_absorb = restrict_pair(residue, absorption, True)
    coarse_source = 4.0 * coarse_source
    coarse_absorb = 4.0 * coarse_absorb
    if depth_level + 1 < agglomerate_level:
        correction = fine_cycle(depth_level + 1, coarse_source, coarse_absorb)
    else:
        correction = agglomerate(coarse_source, coarse_absorb)
    field = field + prolong_field(correction, True)
    field = chebyshev(field, source, diagonal, operate)
    return field


def per_device(right_side, absorption):
    return fine_cycle(0, right_side, absorption)


def solution(mesh):
    in_specs = (P("gx", "gy", None), P("gx", "gy", None))
    out_specs = P("gx", "gy", None)
    return jax.shard_map(
        per_device, mesh=mesh, in_specs=in_specs, out_specs=out_specs, check_vma=False
    )
```

profile of v0, /device:TPU:1, one launch (start us, length us, event | category | flops | bytes accessed | tf_op | source)
XLA Modules:
  0.0 971.8 jit_solution(10794916410311754263)
XLA Ops:
  2.8 4.5 collective-permute-start
  104.0 4.4 collective-permute-done.16
  129.8 13.0 %slice.2145 = f32[16,16,256]{2,1,0:T(8,128)} slice(f32[16,16,512]{2,1,0:T(8,128)} %multiply_add_fusion.7), slice={[0:16:1], [0:16:1], [1:512:2]} | slice | bytes 524288 | tf_op jit(solution)/shard_map/slice | solution.py:78
  142.8 13.0 %slice.2144 = f32[16,16,256]{2,1,0:T(8,128)} slice(f32[16,16,512]{2,1,0:T(8,128)} %multiply_add_fusion.7), slice={[0:16:1], [0:16:1], [0:512:2]} | slice | bytes 524288 | tf_op jit(solution)/shard_map/slice | solution.py:77
  162.0 12.2 %slice.2152 = f32[16,16,256]{2,1,0:T(8,128)} slice(f32[16,16,512]{2,1,0:T(8,128)S(1)} %multiply_add_fusion.6), slice={[0:16:1], [0:16:1], [1:512:2]} | slice | bytes 524288 | tf_op jit(solution)/shard_map/slice | solution.py:78
  174.2 12.2 %slice.2151 = f32[16,16,256]{2,1,0:T(8,128)} slice(f32[16,16,512]{2,1,0:T(8,128)S(1)} %multiply_add_fusion.6), slice={[0:16:1], [0:16:1], [0:512:2]} | slice | bytes 524288 | tf_op jit(solution)/shard_map/slice | solution.py:77
  188.1 12.7 %slice.2146 = f32[16,16,256]{2,1,0:T(8,128)S(1)} slice(f32[16,16,513]{2,1,0:T(8,128)} %concatenate.350), slice={[0:16:1], [0:16:1], [2:513:2]} | slice | bytes 524288 | tf_op jit(solution)/shard_map/slice | solution.py:79
  200.8 12.5 %slice.2153 = f32[16,16,256]{2,1,0:T(8,128)S(1)} slice(f32[16,16,513]{2,1,0:T(8,128)} %concatenate.352), slice={[0:16:1], [0:16:1], [2:513:2]} | slice | bytes 524288 | tf_op jit(solution)/shard_map/slice | solution.py:79
  222.4 4.4 collective-permute-start.20
  245.6 5.3 collective-permute-done.25
  260.0 5.7 collective-permute-start.28
  331.8 5.7 collective-permute-start.42
  387.3 22.0 %all_gather.7 = f32[4,64,64]{2,0,1:T(4,128)S(1)} all-gather(f32[4,4,64]{2,0,1:T(4,128)S(1)} %copy.293), channel_id=1, replica_groups=mesh['gx'=8,'gy'=16] {'gy'}, dimensions={1}, use_global_device_ids=true | all-gather | bytes 69632 | tf_op jit(solution)/shard_map/all_gather | solution.py:142
  409.3 16.9 %all_gather.6 = f32[4,64,64]{2,0,1:T(4,128)S(1)} all-gather(f32[4,4,64]{2,0,1:T(4,128)S(1)} %copy.292), channel_id=1, replica_groups=mesh['gx'=8,'gy'=16] {'gy'}, dimensions={1}, use_global_device_ids=true | all-gather | bytes 69632 | tf_op jit(solution)/shard_map/all_gather | solution.py:141
  426.2 13.5 %collective-permute-start.54 = (f32[1,64,64]{2,1,0:T(8,128)S(1)}, f32[1,64,64]{2,1,0:T(8,128)S(1)}, u32[]{:S(2)}, u32[]{:S(2)}) collective-permute-start(f32[1,64,64]{2,1,0:T(8,128)S(1)} %get-tuple-element.127), channel_id=1, source_target_pairs={{0,16},{16,32},{32,48},{48,64},{64,80},{80,96},{96,112},{1,17},{17... | collective-permute-start | bytes 49160 | tf_op jit(solution)/shard_map/ppermute | solution.py:24
  679.2 4.6 collective-permute-start.106
  709.3 5.5 collective-permute-done.113
  723.1 5.7 collective-permute-start.116
  764.7 5.0 collective-permute-start.124
  810.0 5.7 collective-permute-start.134
  851.8 8.4 copy.339
  860.1 6.3 copy.340
  869.1 5.1 collective-permute-start.142
  927.9 6.2 collective-permute-start.152
  (783 shorter events, 756.7 us)
Async XLA Ops:
  2.8 6.4 collective-permute-start
  7.3 5.6 collective-permute-start.1
  32.4 5.6 collective-permute-start.5
  102.1 6.3 collective-permute-start.16
  110.6 11.1 %collective-permute-start.17 = (f32[2,16,1,512]{3,2,1,0:T(1,128)S(1)}, f32[2,16,1,512]{3,2,1,0:T(1,128)S(1)}, u32[]{:S(2)}, u32[]{:S(2)}) collective-permute-start(f32[2,16,1,512]{3,2,1,0:T(1,128)S(1)} %pad_maximum_fusion.45), channel_id=1, source_target_pairs={{1,0},{2,1},{3,2},{4,3},{5,4},{6,5},{7,6},{8,7},{9,8},{10,9},{11,1... | collective-permute-start | bytes 196616 | tf_op jit(solution)/shard_map/ppermute | solution.py:33
  216.6 5.7 collective-permute-start.19
  222.4 5.7 collective-permute-start.20
  244.3 6.6 collective-permute-start.25
  260.0 7.1 collective-permute-start.28
  331.8 7.1 collective-permute-start.42
  426.2 15.5 %collective-permute-start.54 = (f32[1,64,64]{2,1,0:T(8,128)S(1)}, f32[1,64,64]{2,1,0:T(8,128)S(1)}, u32[]{:S(2)}, u32[]{:S(2)}) collective-permute-start(f32[1,64,64]{2,1,0:T(8,128)S(1)} %get-tuple-element.127), channel_id=1, source_target_pairs={{0,16},{16,32},{32,48},{48,64},{64,80},{80,96},{96,112},{1,17},{17... | collective-permute-start | bytes 49160 | tf_op jit(solution)/shard_map/ppermute | solution.py:24
  538.5 6.1 collective-permute-start.75
  545.6 6.1 collective-permute-start.76
  562.2 6.1 collective-permute-start.80
  578.0 6.1 collective-permute-start.84
  593.6 5.8 collective-permute-start.87
  635.1 5.9 collective-permute-start.96
  679.2 6.6 collective-permute-start.106
  708.0 6.8 collective-permute-start.113
  723.1 7.1 collective-permute-start.116
  764.7 7.0 collective-permute-start.124
  810.0 7.1 collective-permute-start.134
  869.1 7.0 collective-permute-start.142
  927.9 7.8 collective-permute-start.152
  (143 other events, 729.1 us)
where the time goes:
time: 985 us; the launch traced here: 972 us
  starting transfers between devices  419 us (43%)
  waiting for transfers between devices  256 us (26%)
  local copies, waits for them, and re-layouts  156 us (16%)
  other arithmetic  97.3 us (10%)
  blocking collectives  38.8 us (4%)
    ppermute x71, starting transfers between devices, padded_2(): before = lax.ppermute(last, axis, up)  254 us
    ppermute x71, waiting for transfers between devices, padded_2(): after = lax.ppermute(first, axis, down)  222 us
    ppermute x71, starting transfers between devices, padded_2(): after = lax.ppermute(first, axis, down)  129 us
    slice x20, local copies, waits for them, and re-layouts, restrict_dim(): last = lax.slice_in_dim(joined, 2, count + 1, 2, dim)  39.7 us
    slice x20, local copies, waits for them, and re-layouts, restrict_dim(): first = lax.slice_in_dim(joined, 0, count, 2, dim)  38.3 us
    slice x20, local copies, waits for them, and re-layouts, restrict_dim(): middle = lax.slice_in_dim(joined, 1, count, 2, dim)  36.5 us
    ppermute x16, starting transfers between devices, from_behind(): return lax.ppermute(block, axis, route)  36 us
    concatenate x47, other arithmetic, padded_2(): value = jnp.concatenate([before, value, after], axis=dim)  31.9 us
  transfers between devices with their start and end apart: 158, of which 86 were waited for; matrix products, arithmetic and copies ran while one was open for 1% of the time, Pallas kernels for 0%

commit v1 on v0

v1 whole, which is shorter than its diff:
```python
import jax
import jax.numpy as jnp
from jax import lax
from jax.experimental import pallas as pl
from jax.experimental.pallas import tpu as pltpu
from jax.sharding import PartitionSpec as P

MESH = pl.DeviceIdType.MESH
CENTER = 0.7875
HALF = 0.6125
GX, GY = 8, 16
X0, Y0 = 4, 12
LO, UP = 4, 5
B = (32, 16, 8)
ZT = (4, 2, 1)
ROWS = (56, 40, 40)
CH = (5, 3, 2)
DIRS = [(dx, dy) for dx in (-1, 0, 1) for dy in (-1, 0, 1) if dx or dy]
F32 = jnp.float32


def chebyshev_factors():
    out, q = [], HALF / CENTER
    for _ in range(3):
        n = 1.0 / (2.0 * CENTER / HALF - q)
        out.append((n * q, 2.0 * n / HALF))
        q = n
    return out


FACTORS = chebyshev_factors()


def device(dx, dy):
    return (
        lax.rem(lax.axis_index("gx") + (dx + GX), GX),
        lax.rem(lax.axis_index("gy") + (dy + GY), GY),
    )


def dot(a, b):
    return jnp.dot(a, b, precision=lax.Precision.HIGHEST, preferred_element_type=F32)


def spans(way, width, lo, up, start):
    if way == 0:
        return (start, width), (start, width)
    if way > 0:
        return (start + width - lo, lo), (start - lo, lo)
    return (start, up), (start + width, up)


class Exchange:
    def __init__(self, ref, width, lo, up, send, recv, slot):
        self.copies = []
        for n, (dx, dy) in enumerate(DIRS):
            (sx, nx), (tx, _) = spans(dx, width, lo, up, X0)
            (sy, ny), (ty, _) = spans(dy, width, lo, up, Y0)
            self.copies.append(
                pltpu.make_async_remote_copy(
                    src_ref=ref.at[pl.ds(sx, nx), :, pl.ds(sy, ny), :],
                    dst_ref=ref.at[pl.ds(tx, nx), :, pl.ds(ty, ny), :],
                    send_sem=send.at[slot, n],
                    recv_sem=recv.at[slot, n],
                    device_id=device(dx, dy),
                    device_id_type=MESH,
                )
            )

    def start(self):
        for c in self.copies:
            c.start()
        return self

    def wait_recv(self):
        for c in self.copies:
            c.wait_recv()

    def wait_send(self):
        for c in self.copies:
            c.wait_send()


def zero_outside(ref, width, lower=True, upper=True):
    gx, gy = lax.axis_index("gx"), lax.axis_index("gy")

    def clear(cond, planes, rows):
        @pl.when(cond)
        def _():
            view = (pl.ds(*planes), slice(None), pl.ds(*rows), slice(None))
            ref[view] = jnp.zeros((planes[1], ref.shape[1], rows[1], 128), F32)

    whole_x, whole_y = (0, X0 + width + UP), (8, width + 9)
    if lower:
        clear(gx == 0, (0, X0), whole_y)
        clear(gy == 0, whole_x, (8, 4))
    if upper:
        clear(gx == GX - 1, (X0 + width, UP), whole_y)
        clear(gy == GY - 1, whole_x, (Y0 + width, UP))


def lanes_of(u):
    return lax.broadcasted_iota(jnp.int32, u.shape, u.ndim - 1)


def z_split(u):
    lane = lanes_of(u)
    left, right = pltpu.roll(u, 1, axis=2), pltpu.roll(u, 127, axis=2)
    zero = jnp.zeros_like(u[:1])
    if u.shape[0] > 1:
        before = jnp.concatenate([zero, left[:-1]], 0)
        after = jnp.concatenate([right[1:], zero], 0)
    else:
        before = after = zero
    return u + jnp.where(lane == 0, before, left) + jnp.where(lane == 127, after, right)


def z_halves(u):
    lane = lanes_of(u) & 63
    left, right = pltpu.roll(u, 1, axis=2), pltpu.roll(u, 127, axis=2)
    return u + jnp.where(lane == 0, 0.0, left) + jnp.where(lane == 63, 0.0, right)


def z_open(u):
    return u + pltpu.roll(u, 1, axis=2) + pltpu.roll(u, 127, axis=2)


def x_plain(p, n):
    out = []
    for k in range(0, n, 2):
        m = p[k + 1] + p[k + 2] if k + 1 < n else p[k + 1] + p[k + 2]
        out.append(p[k] + m)
        if k + 1 < n:
            out.append(m + p[k + 3])
    return out


def x_pairs(p, n):
    w = [pltpu.roll(v, 64, axis=2) for v in p]
    low = lanes_of(p[0]) < 64
    return [p[k + 1] + w[k + 1] + jnp.where(low, w[k], w[k + 2]) for k in range(n)]


def smooth_step(lev, src, r, x_range, dst=None, al=0.0, be=0.0, r_out=None, extra=None):
    gi, tmp = lev["gi"], lev["tmp"]
    rows = 8 * (lev["ch"] + 2)

    def group(x, n):
        p = [src[x - 1 + k, :, 0:rows, :] for k in range(n + 2)]
        for k, s in enumerate(lev["xsum"](p, n)):
            tmp[k] = s
        for k in range(n):
            for c in range(lev["ch"]):
                a = 8 + 8 * c
                u = tmp[k, :, a - 1 : a + 7, :] + tmp[k, :, a : a + 8, :] + tmp[k, :, a + 1 : a + 9, :]
                box = lev["zsum"](u)
                d = src[x + k, :, a : a + 8, :]
                new = (r[x + k, :, a : a + 8, :] - d) + gi[x + k, :, a : a + 8, :] * (box - d)
                if extra is not None:
                    extra(x + k, a, d, new)
                if r_out is not None:
                    r_out[x + k, :, a : a + 8, :] = new
                if dst is not None:
                    dst[x + k, :, a : a + 8, :] = al * d + be * new

    first, last = x_range
    size = tmp.shape[0]
    full = (last - first) // size
    rest = (last - first) - full * size
    if full == 1:
        group(first, size)
    elif full:
        def body(i, carry):
            group(first + i * size, size)
            return carry
        lax.fori_loop(0, full, body, 0)
    if rest:
        group(first + full * size, rest)


def begin(lev, f, s, planes, chunks, mask):
    gi, r, d = lev["gi"], lev["r"], lev["d"][0]

    def body(x, carry):
        for c in range(chunks):
            a = 8 + 8 * c
            g = mask(1.0 / (26.0 + s[x, :, a : a + 8, :]), x, a)
            gi[x, :, a : a + 8, :] = g
            new = f[x, :, a : a + 8, :] * g
            r[x, :, a : a + 8, :] = new
            d[x, :, a : a + 8, :] = new * (1.0 / CENTER)
        return carry

    lax.fori_loop(planes[0], planes[1], body, 0)


def store_own(ref, x, a, value, width):
    lo, hi = max(a, Y0), min(a + 8, Y0 + width)
    if lo < hi:
        ref[x, :, lo:hi, :] = value[:, lo - a : hi - a, :]


def restrict_rows(src, tmp, out, count, cy, first_plane, first_row, rows):
    size = min(4, count)

    def body(i, carry):
        for k in range(size):
            x = first_plane + 2 * (i * size + k)
            tmp[k] = 0.25 * (src[x, :, 0:rows, :] + src[x + 2, :, 0:rows, :]) + 0.5 * src[x + 1, :, 0:rows, :]
        for k in range(size):
            for z in range(src.shape[1]):
                v = 0.25 * (
                    tmp[k, z, pl.ds(first_row, cy, stride=2), :]
                    + tmp[k, z, pl.ds(first_row + 2, cy, stride=2), :]
                ) + 0.5 * tmp[k, z, pl.ds(first_row + 1, cy, stride=2), :]
                at = (i * size + k) * cy
                if cy % 8 == 0:
                    at = pl.multiple_of(at, 8)
                out[z, pl.ds(at, cy), :] = v
        return carry

    lax.fori_loop(0, count // size, body, 0)


def split_restrict(level, src, tmp, mid, matrix, target):
    cb = B[level + 1]
    restrict_rows(src, tmp, mid, cb, cb, X0, Y0, 8 * (CH[level] + 2))
    total = None
    for z in range(ZT[level]):
        part = dot(mid[z], matrix[z])
        total = part if total is None else total + part
    for i in range(cb):
        for z in range(ZT[level + 1]):
            target[X0 + i, z, Y0 : Y0 + cb, :] = total[i * cb : (i + 1) * cb, 128 * z : 128 * z + 128]


def interleave(ez, target, count, t0, rows, nj, first_plane, first_row):
    for_z = range(target.shape[1])

    def body(i, carry):
        t = t0 + i
        for z in for_z:
            a1, b1 = ez[t, z, rows : rows + nj, :], ez[t, z, rows - 1 : rows - 1 + nj, :]
            a0, b0 = ez[t - 1, z, rows : rows + nj, :], ez[t - 1, z, rows - 1 : rows - 1 + nj, :]
            odd, even = a1, 0.5 * (a1 + b1)
            odd_0, even_0 = a0, 0.5 * (a0 + b0)
            x = first_plane + 2 * i
            target[x, z, pl.ds(first_row + 1, nj, stride=2), :] = 0.5 * (odd_0 + odd)
            target[x, z, pl.ds(first_row, nj, stride=2), :] = 0.5 * (even_0 + even)
            target[x + 1, z, pl.ds(first_row + 1, nj, stride=2), :] = odd
            target[x + 1, z, pl.ds(first_row, nj, stride=2), :] = even
        return carry

    lax.fori_loop(0, count, body, 0)


def kernel(f_hbm, s_hbm, out_hbm, *refs):
    it = iter(refs)
    lev = []
    for l in range(3):
        me = dict(ch=CH[l], xsum=x_plain, zsum=z_split)
        for name in ("r", "s", "rho", "tmp", "mid") + (("e",) if l else ()):
            me[name] = next(it)
        if l == 1:
            old = lev[0]["d"]
            views = [old[n].at[pl.ds(0, 25), pl.ds(z, 2), pl.ds(0, 40), :] for n in (2, 3, 1) for z in (0, 2)]
            me["d"], me["gi"], me["x"] = views[:4], views[4], views[5]
        else:
            me["d"] = [next(it) for _ in range(4)]
            me["gi"], me["x"] = next(it), next(it)
        me["ez"] = me["d"][1].at[pl.ds(0, 21), :, pl.ds(0, 32), :] if l == 0 else next(it)
        lev.append(me)
    for l in range(3, 6):
        me = dict(ch=(8, 4, 2)[l - 3], xsum=x_pairs if l == 3 else x_plain, zsum=z_halves if l == 3 else z_open)
        for name in ("gi", "tmp", "mid", "ez"):
            me[name] = next(it)
        if l == 4:
            old = lev[0]["r"]
            fields = [old.at[pl.ds(x, 18), pl.ds(z, 1), pl.ds(0, 48), :] for x in (0, 18) for z in range(4)]
        else:
            fields = [next(it) for _ in range(8)]
        me["d"] = fields[:4]
        me["r"], me["s"], me["x"], me["f"] = fields[4:]
        lev.append(me)
    blk_f, blk_s = next(it), next(it)
    rz0, pz0, rz1, pz1, rz2, pz2, rz3, pz3, rz4, pz4 = [next(it) for _ in range(10)]
    load_sem, send, recv, gsend, grecv = [next(it) for _ in range(5)]
    gx, gy = lax.axis_index("gx"), lax.axis_index("gy")

    loads = []
    for n, (hbm, ref) in enumerate(((s_hbm, lev[0]["s"]), (f_hbm, lev[0]["r"]))):
        for z in range(4):
            c = pltpu.make_async_copy(
                hbm.at[:, :, pl.ds(128 * z, 128)], ref.at[pl.ds(X0, 32), z, pl.ds(Y0, 32), :], load_sem.at[n, z]
            )
            c.start()
            loads.append(c)

    def clear_pads(l):
        for ref in lev[l]["d"] + [lev[l]["r"], lev[l]["s"], lev[l]["x"]]:
            rows = ref.shape[2]
            top = 8 + 8 * lev[l]["ch"]
            off = 2 if l == 3 else 1
            n = ref.shape[0]
            ref[0:off] = jnp.zeros((off,) + ref.shape[1:], F32)
            ref[n - off : n] = jnp.zeros((off,) + ref.shape[1:], F32)
            ref[:, :, 0:8, :] = jnp.zeros((n, 1, 8, 128), F32)
            ref[:, :, top:rows, :] = jnp.zeros((n, 1, rows - top, 128), F32)
        ez = lev[l]["ez"]
        ez[...] = jnp.zeros(ez.shape, F32)
        mid = lev[l]["mid"]
        mid[...] = jnp.zeros(mid.shape, F32)

    clear_pads(3)
    clear_pads(5)

    barrier = pltpu.get_barrier_semaphore()
    peers = list(DIRS) + [(d, 0) for d in range(2, GX - 1)] + [(0, d) for d in range(2, GY - 1)]
    for dx, dy in peers:
        pl.semaphore_signal(barrier, inc=1, device_id=device(dx, dy), device_id_type=MESH)
    pl.semaphore_wait(barrier, len(peers))

    for c in loads[:4]:
        c.wait()
    slot = iter(range(16))

    def exchange(ref, l, lo, up):
        return Exchange(ref, B[l], lo, up, send, recv, next(slot)).start()

    sends = []
    ex_s = [exchange(lev[0]["s"], 0, LO, UP)]
    for c in loads[4:]:
        c.wait()
    ex_f = exchange(lev[0]["r"], 0, LO, UP)

    def fill(ref, index, fn):
        shape = ref.shape[1:]
        ref[index] = fn(lax.broadcasted_iota(jnp.int32, shape, 0), lax.broadcasted_iota(jnp.int32, shape, 1))

    def wr(z, k):
        return jnp.where(z == 2 * k + 1, 2.0, jnp.where((z == 2 * k) | (z == 2 * k + 2), 1.0, 0.0))

    def wp(k, z):
        return jnp.where(z == 2 * k + 1, 1.0, jnp.where((z == 2 * k) | (z == 2 * k + 2), 0.5, 0.0))

    for t in range(4):
        fill(rz0, t, lambda z, k: wr(z + 128 * t, k))
    for t in range(2):
        fill(pz0, t, lambda k, z: wp(k + 128 * t, z))
        fill(rz1, t, lambda z, k: wr(z + 128 * t, k))
    fill(pz1, 0, wp)
    for h in range(2):
        fill(rz2, h, lambda z, k: jnp.where((k >> 6) == h, wr(z, k & 63), 0.0))
        fill(pz2, h, lambda k, z: jnp.where((k >> 6) == h, wp(k & 63, z), 0.0))
    fill(rz3, 0, lambda z, k: jnp.where(k < 32, wr(z & 63, k) * jnp.where(z < 64, 0.25, 0.5), 0.0))
    fill(rz3, 1, lambda z, k: jnp.where((k < 32) & (z < 64), wr(z, k) * 0.25, 0.0))
    fill(pz3, 0, lambda k, z: jnp.where(k < 32, wp(k, z & 63) * jnp.where(z < 64, 0.5, 1.0), 0.0))
    fill(pz3, 1, lambda k, z: jnp.where((k < 32) & (z < 64), wp(k, z) * 0.5, 0.0))
    fill(rz4, 0, lambda z, k: jnp.where((k < 16) & (z < 32), wr(z, k), 0.0))
    fill(pz4, 0, lambda k, z: jnp.where((k < 16) & (z < 32), wp(k, z), 0.0))
    rz, pz = (rz0, rz1), (pz0, pz1)

    def pack_block(l2, src, blk):
        mid = l2["mid"]
        restrict_rows(src, l2["tmp"], mid, 4, 4, X0, Y0, 32)
        lo, hi = dot(mid[0], rz2[0]), dot(mid[0], rz2[1])
        for i in range(2):
            blk[i, 0, 0:4, :] = lo[8 * i : 8 * i + 4] + hi[8 * i + 4 : 8 * i + 8]

    class Gather:
        def __init__(self, n, blk, ref):
            own = ref.at[pl.ds(2 + 2 * gx, 2), :, pl.ds(8 + 4 * gy, 4), :]
            src = blk.at[:, :, pl.ds(0, 4), :]
            self.local = pltpu.make_async_copy(src, own, load_sem.at[2, n])
            slab = ref.at[pl.ds(2, 16), :, pl.ds(8 + 4 * gy, 4), :]
            self.first = [
                pltpu.make_async_remote_copy(
                    src_ref=src, dst_ref=own, send_sem=gsend.at[n, d], recv_sem=grecv.at[n, d],
                    device_id=device(d, 0), device_id_type=MESH)
                for d in range(1, GX)
            ]
            self.second = [
                pltpu.make_async_remote_copy(
                    src_ref=slab, dst_ref=slab, send_sem=gsend.at[n, 8 + d], recv_sem=grecv.at[n, 8 + d],
                    device_id=device(0, d), device_id_type=MESH)
                for d in range(1, GY)
            ]

        def start(self):
            for c in self.first:
                c.start()
            self.local.start()

        def middle(self):
            self.local.wait()
            for c in self.first:
                c.wait_recv()
            for c in self.second:
                c.start()

        def finish(self):
            for c in self.second:
                c.wait_recv()

        def wait_send(self):
            for c in self.first + self.second:
                c.wait_send()

    gather_s = Gather(0, blk_s, lev[3]["s"])
    gather_f = Gather(1, blk_f, lev[3]["f"])

    def edge_mask(l):
        row_lo = jnp.where(gy == 0, Y0, 0)
        row_hi = jnp.where(gy == GY - 1, Y0 + B[l], 1000)
        x_lo = jnp.where(gx == 0, X0, 0)
        x_hi = jnp.where(gx == GX - 1, X0 + B[l], 1000)

        def mask(v, x, a):
            row = lax.broadcasted_iota(jnp.int32, v.shape, 1) + a
            inside = (row >= row_lo) & (row < row_hi) & (x >= x_lo) & (x < x_hi)
            return jnp.where(inside, v, 0.0)

        return mask

    def pre(l, between):
        me, b = lev[l], B[l]
        begin(me, me["r"], me["s"], (0, b + 9), me["ch"] + 1, edge_mask(l))
        d, r = me["d"], me["r"]
        for k in range(3):
            al, be = FACTORS[k]
            smooth_step(me, d[k], r, (X0 - 3 + k, X0 + b + 4 - k), d[k + 1], al, be, r_out=r)
            between(k)

        def residual(x, a, _, new):
            r[x, :, a : a + 8, :] = (26.0 + me["s"][x, :, a : a + 8, :]) * new

        def extra(x, a, dd, new):
            residual(x, a, dd, new)
            store_own(me["rho"], x, a, new, b)
            me["x"][x - X0, :, a : a + 8, :] = (
                (d[0][x, :, a : a + 8, :] + d[1][x, :, a : a + 8, :]) + d[2][x, :, a : a + 8, :]
            ) + dd

        smooth_step(me, d[3], r, (X0, X0 + b), extra=extra)
        smooth_step(me, d[3], r, (X0 + b, X0 + b + 1), extra=residual)

    def post(l, emit):
        me, b = lev[l], B[l]
        d, rho = me["d"], me["rho"]
        smooth_step(me, d[0], rho, (X0 - 3, X0 + b + 3), d[1], 0.0, 1.0 / CENTER, r_out=rho)
        smooth_step(me, d[1], rho, (X0 - 2, X0 + b + 2), d[2], *FACTORS[0], r_out=rho)
        smooth_step(me, d[2], rho, (X0 - 1, X0 + b + 1), d[3], *FACTORS[1], r_out=rho)
        al, be = FACTORS[2]

        def extra(x, a, dd, new):
            s = slice(a, a + 8)
            total = (me["x"][x - X0, :, s, :] + d[0][x, :, s, :]) + (d[1][x, :, s, :] + d[2][x, :, s, :])
            emit(x, a, (total + dd) + (al * dd + be * new))

        smooth_step(me, d[3], rho, (X0, X0 + b), extra=extra)

    def coarse_s(k):
        if k < 2:
            ex_s[k + 1].wait_recv()
            zero_outside(lev[k + 1]["s"], B[k + 1])
        if k == 0:
            split_restrict(1, lev[1]["s"], lev[1]["tmp"], lev[1]["mid"], rz[1], lev[2]["s"])
            ex_s.append(exchange(lev[2]["s"], 2, LO, UP))
        elif k == 1:
            pack_block(lev[2], lev[2]["s"], blk_s)
            gather_s.start()
        else:
            gather_s.middle()

    ex_s[0].wait_recv()
    zero_outside(lev[0]["s"], 32)
    split_restrict(0, lev[0]["s"], lev[0]["tmp"], lev[0]["mid"], rz[0], lev[1]["s"])
    ex_s.append(exchange(lev[1]["s"], 1, LO, UP))

    ex_rho = []
    for l in range(3):
        ex_f.wait_recv()
        ex_f.wait_send()
        pre(l, coarse_s if l == 0 else lambda k: None)
        ex_rho.append(exchange(lev[l]["rho"], l, 3, 3))
        if l < 2:
            split_restrict(l, lev[l]["r"], lev[l]["tmp"], lev[l]["mid"], rz[l], lev[l + 1]["r"])
            ex_f = exchange(lev[l + 1]["r"], l + 1, LO, UP)
    pack_block(lev[2], lev[2]["r"], blk_f)
    gather_f.start()
    clear_pads(4)
    gather_f.middle()
    gather_s.finish()
    gather_f.finish()

    def whole_pre(l, off, planes):
        me = lev[l]
        d, r = me["d"], me["r"]
        lanes = (128, 32, 16)[l - 3]

        def mask(v, x, a):
            return v if lanes == 128 else jnp.where(lanes_of(v) < lanes, v, 0.0)

        begin(me, me["f"], me["s"], (off, off + planes), me["ch"], mask)
        for k in range(3):
            al, be = FACTORS[k]
            smooth_step(me, d[k], r, (off, off + planes), d[k + 1], al, be, r_out=r)

    def whole_residual(l, off, planes, f):
        me = lev[l]
        d, r = me["d"], me["r"]

        def extra(x, a, dd, new):
            s = slice(a, a + 8)
            me["x"][x, :, s, :] = ((d[0][x, :, s, :] + d[1][x, :, s, :]) + d[2][x, :, s, :]) + dd
            f[x, :, s, :] = (26.0 + me["s"][x, :, s, :]) * new

        smooth_step(me, d[3], r, (off, off + planes), r_out=r, extra=extra)

    def whole_post(l, off, planes):
        me = lev[l]
        d, r = me["d"], me["r"]
        span = (off, off + planes)
        smooth_step(me, d[0], r, span, d[1], 0.0, 1.0 / CENTER, r_out=r)
        smooth_step(me, d[1], r, span, d[2], *FACTORS[0], r_out=r)
        smooth_step(me, d[2], r, span, d[3], *FACTORS[1], r_out=r)
        al, be = FACTORS[2]

        def extra(x, a, dd, new):
            s = slice(a, a + 8)
            total = (me["x"][x, :, s, :] + d[0][x, :, s, :]) + (d[1][x, :, s, :] + d[2][x, :, s, :])
            me["x"][x, :, s, :] = (total + dd) + (al * dd + be * new)

        smooth_step(me, d[3], r, span, extra=extra)

    l3, l4, l5 = lev[3], lev[4], lev[5]
    whole_pre(3, 2, 16)
    whole_residual(3, 2, 16, l3["d"][0])

    def down_pairs(src, target):
        mid = l3["mid"]

        def body(i, carry):
            v = 0.25 * (src[2 + i, 0, pl.ds(8, 32, stride=2), :] + src[2 + i, 0, pl.ds(10, 32, stride=2), :])
            mid[0, pl.ds(pl.multiple_of(32 * i, 8), 32), :] = v + 0.5 * src[2 + i, 0, pl.ds(9, 32, stride=2), :]
            return carry

        lax.fori_loop(0, 16, body, 0)
        total = dot(mid[0, 0:512, :], rz3[0]) + dot(mid[0, 32:544, :], rz3[1])
        for i in range(16):
            target[1 + i, 0, 8:40, :] = total[32 * i : 32 * i + 32]

    def down_whole(src, target):
        mid = l4["mid"]
        restrict_rows(src, l4["tmp"], mid, 8, 16, 1, 8, 48)
        total = dot(mid[0], rz4[0])
        for i in range(8):
            target[1 + i, 0, 8:24, :] = total[16 * i : 16 * i + 16]

    down_pairs(l3["s"], l4["s"])
    down_whole(l4["s"], l5["s"])
    down_pairs(l3["d"][0], l4["f"])
    whole_pre(4, 1, 16)
    whole_residual(4, 1, 16, l4["d"][0])
    down_whole(l4["d"][0], l5["f"])

    whole_pre(5, 1, 8)
    d5, r5 = l5["d"], l5["r"]

    def turn(x, a, dd, new):
        s = slice(a, a + 8)
        l5["x"][x, :, s, :] = ((d5[0][x, :, s, :] + d5[1][x, :, s, :]) + d5[2][x, :, s, :]) + dd

    smooth_step(l5, d5[3], r5, (1, 9), d5[0], 0.0, 1.0 / CENTER, r_out=r5, extra=turn)
    for k in range(2):
        smooth_step(l5, d5[k], r5, (1, 9), d5[k + 1], *FACTORS[k], r_out=r5)
    al, be = FACTORS[2]

    def last(x, a, dd, new):
        s = slice(a, a + 8)
        total = (l5["x"][x, :, s, :] + d5[0][x, :, s, :]) + d5[1][x, :, s, :]
        l5["x"][x, :, s, :] = (total + dd) + (al * dd + be * new)

    smooth_step(l5, d5[2], r5, (1, 9), extra=last)

    up = dot(l5["x"][1:9, 0, 8:24, :].reshape(128, 128), pz4[0])
    for i in range(8):
        l4["ez"][1 + i, 0, 8:24, :] = up[16 * i : 16 * i + 16]
    interleave(l4["ez"], l4["d"][0], 8, 1, 8, 16, 1, 8)
    whole_post(4, 1, 16)

    e4 = l4["x"]
    up = dot(e4[1:17, 0, 8:40, :].reshape(512, 128), pz3[0]) + dot(e4[0:16, 0, 8:40, :].reshape(512, 128), pz3[1])
    for i in range(16):
        l3["ez"][i, 0, 8:40, :] = up[32 * i : 32 * i + 32]

    def rows_up(i, carry):
        a, b = l3["ez"][i, 0, 8:40, :], l3["ez"][i, 0, 7:39, :]
        l3["d"][0][2 + i, 0, pl.ds(9, 32, stride=2), :] = a
        l3["d"][0][2 + i, 0, pl.ds(8, 32, stride=2), :] = 0.5 * (a + b)
        return carry

    lax.fori_loop(0, 16, rows_up, 0)
    whole_post(3, 2, 16)

    def clear_top(l):
        zero_outside(lev[l]["d"][0], B[l], lower=False)

    def correct(l):
        ex_rho[l].wait_recv()
        ex_rho[l].wait_send()
        zero_outside(lev[l]["rho"], B[l])

    win = l3["x"][pl.ds(2 * gx, 5), 0, pl.ds(4 * gy + 4, 24), :].reshape(120, 128)
    for h in range(2):
        up = dot(win, pz2[h])
        for m in range(5):
            lev[2]["ez"][2 * m + h, 0] = up[24 * m : 24 * m + 24]
    interleave(lev[2]["ez"], lev[2]["d"][0], 8, 2, 2, 16, 0, 8)
    clear_top(2)
    correct(2)
    post(2, lambda x, a, v: store_own(lev[2]["e"], x, a, v, 8))

    for l in (1, 0):
        e = lev[l + 1]["e"]
        ex_e = exchange(e, l + 1, 3, 2)
        sends.append(ex_e)
        correct(l)
        ex_e.wait_recv()
        zero_outside(e, B[l + 1], upper=False)
        ez = lev[l]["ez"]
        er = ez.shape[2]
        step = 7 if l == 0 else 13
        for t in range(0, ez.shape[0], step):
            total = None
            for z in range(ZT[l + 1]):
                v = e[1 + t : 1 + t + step, z, 8 : 8 + er, :].reshape(step * er, 128)
                part = dot(v, pz[l][z])
                total = part if total is None else total + part
            for k in range(step):
                for z in range(ZT[l]):
                    ez[t + k, z] = total[er * k : er * k + er, 128 * z : 128 * z + 128]
        interleave(ez, lev[l]["d"][0], B[l + 1] + 4, 1, 2, (24, 16)[l], 0, 8)
        clear_top(l)
        if l:
            post(l, lambda x, a, v: store_own(lev[1]["e"], x, a, v, 16))
        else:
            def emit(x, a, v):
                lev[0]["x"][x - X0, :, a : a + 8, :] = v
            post(0, emit)

    stores = [
        pltpu.make_async_copy(
            lev[0]["x"].at[:, z, pl.ds(Y0, 32), :], out_hbm.at[:, :, pl.ds(128 * z, 128)], load_sem.at[3, z]
        )
        for z in range(4)
    ]
    for c in stores:
        c.start()
    for ex in ex_s + sends + [gather_s, gather_f]:
        ex.wait_send()
    for c in stores:
        c.wait()


def per_device(right_side, absorption):
    scratch = []

    def vmem(*shape):
        scratch.append(pltpu.VMEM(shape, F32))

    for l in range(3):
        b, zt, rows = B[l], ZT[l], ROWS[l]
        for _ in range(3):
            vmem(b + 9, zt, rows, 128)
        vmem(8, zt, 8 * (CH[l] + 2), 128)
        vmem(zt, (256, 64, 16)[l], 128)
        if l:
            vmem(b + 9, zt, 40, 128)
        if l != 1:
            for _ in range(5):
                vmem(b + 9, zt, rows, 128)
            vmem(b, zt, rows, 128)
        if l:
            vmem(*((13, 2, 24, 128), (10, 1, 24, 128))[l - 1])
    for l in range(3, 6):
        planes, rows = ((20, 88), (18, 48), (10, 32))[l - 3]
        vmem(planes, 1, rows, 128)
        vmem(8, 1, (80, 48, 32)[l - 3], 128)
        vmem(1, (544, 128, 8)[l - 3], 128)
        vmem(*((16, 1, 48, 128), (9, 1, 32, 128), (1, 1, 8, 128))[l - 3])
        if l != 4:
            for _ in range(8):
                vmem(planes, 1, rows, 128)
    vmem(2, 1, 8, 128)
    vmem(2, 1, 8, 128)
    for shape in ((4, 128, 256), (2, 128, 512), (2, 128, 128), (1, 128, 256), (2, 128, 128), (2, 128, 128),
                  (2, 128, 128), (2, 128, 128), (1, 128, 128), (1, 128, 128)):
        vmem(*shape)
    dma = pltpu.SemaphoreType.DMA
    scratch += [dma((4, 4)), dma((12, 8)), dma((12, 8)), dma((2, 24)), dma((2, 24))]
    return pl.pallas_call(
        kernel,
        out_shape=jax.ShapeDtypeStruct((32, 32, 512), F32),
        in_specs=[pl.BlockSpec(memory_space=pl.ANY)] * 2,
        out_specs=pl.BlockSpec(memory_space=pl.ANY),
        scratch_shapes=scratch,
        compiler_params=pltpu.CompilerParams(
            collective_id=0, has_side_effects=True, vmem_limit_bytes=63 * 2**20
        ),
        name="vcycle",
    )(right_side, absorption)


def solution(mesh):
    spec = P("gx", "gy", None)
    return jax.shard_map(per_device, mesh=mesh, in_specs=(spec, spec), out_specs=spec, check_vma=False)
```

time: 985 us -> 124 us (0.13); the launches traced: 972 us -> 123 us
  starting transfers between devices: 419 us -> 0 us
  waiting for transfers between devices: 256 us -> 0 us
  local copies, waits for them, and re-layouts: 156 us -> 3.19 us
  Pallas kernels: 0 us -> 120 us
  other arithmetic: 97.3 us -> 0 us
  blocking collectives: 38.8 us -> 0 us
    ppermute x158 -> x0, starting transfers between devices: 419 us -> none  [the longest x71 254 us: padded_2(): before = lax.ppermute(last, axis, up)]
    ppermute x158 -> x0, waiting for transfers between devices: 256 us -> none  [the longest x71 222 us: padded_2(): after = lax.ppermute(first, axis, down)]
    pallas_call x0 -> x1, Pallas kernels: none -> 120 us  [per_device(): pl.pallas_call(kernel, out_shape=jax.ShapeDtypeStruct((32, 32, 512), F32)...]
    slice x110 -> x0, local copies, waits for them, and re-layouts: 115 us -> none  [the longest x20 39.7 us: restrict_dim(): last = lax.slice_in_dim(joined, 2, count + 1, 2, dim)]
    add x154 -> x0, other arithmetic: 42.9 us -> none  [the longest x12 10.1 us: chebyshev(): field = update if field is None else field + update]
    all_gather x2 -> x0, blocking collectives: 38.8 us -> none  [the longest x1 22 us: agglomerate(): lax.all_gather(absorption, 'gy', axis=1, tiled=True)]
    concatenate x60 -> x0, other arithmetic: 37.1 us -> none  [the longest x47 31.9 us: padded_2(): value = jnp.concatenate([before, value, after], axis=dim)]
    another operation x33 -> x0, local copies, waits for them, and re-layouts: 16 us -> none  [the longest x19 15.9 us: prolong_dim(): stacked = jnp.stack([even_part, coarse], axis=dim + 1)]
  transfers between devices with their start and end apart: 158 -> 0, of which waited for: 86 -> 0; matrix products, arithmetic and copies ran while one was open for 1% -> 0% of each run, Pallas kernels for 0% -> 0%
where the time goes in v1:
time: 124 us; the launch traced here: 123 us
  Pallas kernels  120 us (97%)
  local copies, waits for them, and re-layouts  3.19 us (3%)
    pallas_call x1, Pallas kernels, per_device(): pl.pallas_call(kernel, out_shape=jax.ShapeDtypeStruct((32, 32, 512), F32)...  120 us
    unnamed x1, local copies, waits for them, and re-layouts  3.19 us

profile of v1, /device:TPU:1, one launch (start us, length us, event | category | flops | bytes accessed | tf_op | source)
XLA Modules:
  0.0 123.5 jit_solution(11619952838408151322)
XLA Ops:
  0.0 120.3 %vcycle.1 = f32[32,32,512]{2,1,0:T(8,128)} custom-call(f32[32,32,512]{2,1,0:T(8,128)} %f_hbm.1, f32[32,32,512]{2,1,0:T(8,128)} %s_hbm.1), custom_call_target="tpu_custom_call" | custom-call | tf_op jit(solution)/shard_map/vcycle/pallas_call | solution.py:702
  120.3 3.2 %copy.4 = f32[32,32,512]{2,1,0:T(8,128)} copy(f32[32,32,512]{2,1,0:T(8,128)} %vcycle.1) | data formatting | bytes 4194304

commit v2 on v1

v2 whole, which is shorter than its diff:
```python
import jax
import jax.numpy as jnp
from jax import lax
from jax.experimental import pallas as pl
from jax.experimental.pallas import tpu as pltpu
from jax.sharding import PartitionSpec as P

MESH = pl.DeviceIdType.MESH
CENTER = 0.7875
HALF = 0.6125
GX, GY = 8, 16
X0, Y0 = (4, 8, 8), (12, 16, 16)
PLANES = (41, 32, 24)
EDGE = (4, 5)
OUTER = ((0, 0), (3, 2), (4, 3))
B = (32, 16, 8)
ZT = (4, 2, 1)
ROWS = (56, 48, 40)
CH = (5, 4, 3)
DIRS = [(dx, dy) for dx in (-1, 0, 1) for dy in (-1, 0, 1) if dx or dy]
F32 = jnp.float32


def chebyshev_factors():
    out, q = [], HALF / CENTER
    for _ in range(3):
        n = 1.0 / (2.0 * CENTER / HALF - q)
        out.append((n * q, 2.0 * n / HALF))
        q = n
    return out


FACTORS = chebyshev_factors()


def device(dx, dy):
    return (
        lax.rem(lax.axis_index("gx") + (dx + GX), GX),
        lax.rem(lax.axis_index("gy") + (dy + GY), GY),
    )


def dot(a, b):
    return jnp.dot(a, b, precision=lax.Precision.HIGHEST, preferred_element_type=F32)


def spans(way, width, lo, up, start):
    if way == 0:
        return (start, width), (start, width)
    if way > 0:
        return (start + width - lo, lo), (start - lo, lo)
    return (start, up), (start + width, up)


def remote(src, dst, send, recv, to):
    return pltpu.make_async_remote_copy(
        src_ref=src, dst_ref=dst, send_sem=send, recv_sem=recv, device_id=device(*to), device_id_type=MESH
    )


class Exchange:
    def __init__(self, ref, level, depth, send, recv, slot, dirs=DIRS):
        self.copies = []
        lo, up = depth
        for n, (dx, dy) in enumerate(dirs):
            (sx, nx), (tx, _) = spans(dx, B[level], lo, up, X0[level])
            (sy, ny), (ty, _) = spans(dy, B[level], lo, up, Y0[level])
            src = ref.at[pl.ds(sx, nx), :, pl.ds(sy, ny), :]
            dst = ref.at[pl.ds(tx, nx), :, pl.ds(ty, ny), :]
            self.copies.append(remote(src, dst, send.at[slot, n], recv.at[slot, n], (dx, dy)))

    def start(self):
        for c in self.copies:
            c.start()
        return self

    def wait_recv(self):
        for c in self.copies:
            c.wait_recv()

    def wait_send(self):
        for c in self.copies:
            c.wait_send()


def zero_outside(ref, level, lower=True, upper=True):
    gx, gy = lax.axis_index("gx"), lax.axis_index("gy")
    x0, y0, b = X0[level], Y0[level], B[level]

    def clear(cond, planes, rows):
        @pl.when(cond)
        def _():
            view = (pl.ds(*planes), slice(None), pl.ds(*rows), slice(None))
            ref[view] = jnp.zeros((planes[1], ref.shape[1], rows[1], 128), F32)

    above = min(8, PLANES[level] - x0 - b)
    whole_x, whole_y = (0, x0 + b + above), (8, y0 + b)
    if lower:
        clear(gx == 0, (0, x0), whole_y)
        clear(gy == 0, whole_x, (8, y0 - 8))
    if upper:
        clear(gx == GX - 1, (x0 + b, above), whole_y)
        clear(gy == GY - 1, whole_x, (y0 + b, 8 if level else 5))


def lanes_of(shape):
    return lax.broadcasted_iota(jnp.int32, shape, len(shape) - 1)


def edges(shape, width):
    lane = lanes_of(shape) & (width - 1)
    return lane == 0, lane == width - 1


def z_split(u, masks):
    left, right = pltpu.roll(u, 1, axis=2), pltpu.roll(u, 127, axis=2)
    zero = jnp.zeros_like(u[:1])
    if u.shape[0] > 1:
        before = jnp.concatenate([zero, left[:-1]], 0)
        after = jnp.concatenate([right[1:], zero], 0)
    else:
        before = after = zero
    return u + lax.select(masks[0], before, left) + lax.select(masks[1], after, right)


def z_open(u, masks):
    return u + pltpu.roll(u, 1, axis=2) + pltpu.roll(u, 127, axis=2)


def x_plain(p, n):
    out = []
    for k in range(0, n, 2):
        m = p[k + 1] + p[k + 2]
        out.append(p[k] + m)
        if k + 1 < n:
            out.append(m + p[k + 3])
    return out


def x_pairs(p, n):
    w = [pltpu.roll(v, 64, axis=2) for v in p]
    low = lanes_of(p[0].shape) < 64
    return [p[k + 1] + w[k + 1] + lax.select(low, w[k], w[k + 2]) for k in range(n)]


def smooth_step(lev, src, r, x_range, dst=None, al=0.0, be=0.0, r_out=None, extra=None, after=None, count=None):
    gi, tmp = lev["gi"], lev["tmp"]
    rows = 8 * (lev["ch"] + 2)

    def group(x, n):
        p = [src[x - 1 + k, :, 0:rows, :] for k in range(n + 2)]
        for k, s in enumerate(lev["xsum"](p, n)):
            tmp[k] = s
        h = lev["tall"]
        masks = edges((tmp.shape[1], h, 128), lev["width"])
        for k in range(n):
            for a in range(8, 8 + 8 * lev["ch"], h):
                s = slice(a, a + h)
                u = tmp[k, :, a - 1 : a + h - 1, :] + tmp[k, :, s, :] + tmp[k, :, a + 1 : a + h + 1, :]
                box = lev["zsum"](u, masks)
                d = src[x + k, :, s, :]
                new = (r[x + k, :, s, :] - d) + gi[x + k, :, s, :] * (box - d)
                if extra is not None:
                    extra(x + k, a, d, new)
                if r_out is not None:
                    r_out[x + k, :, s, :] = new
                if dst is not None:
                    dst[x + k, :, s, :] = al * d + be * new

    first, last = x_range
    size = tmp.shape[0]
    if count is not None:
        group(first, count)
        return
    full = (last - first) // size
    rest = (last - first) - full * size
    if full == 1 and after is None:
        group(first, size)
    elif full:
        def body(i, carry):
            group(first + i * size, size)
            if after is not None:
                after(i, first + i * size)
            return carry
        lax.fori_loop(0, full, body, 0)
    if rest:
        group(first + full * size, rest)


def begin(lev, first, count, chunks, mask):
    gi, r, d, f, s = lev["gi"], lev["r"], lev["d"][0], lev["f"], lev["s"]

    def body(i, carry):
        x = first + i
        rows = slice(8, 8 + 8 * chunks)
        g = mask(1.0 / (26.0 + s[x, :, rows, :]), x)
        gi[x, :, rows, :] = g
        new = f[x, :, rows, :] * g
        r[x, :, rows, :] = new
        d[x, :, rows, :] = new * (1.0 / CENTER)
        return carry

    lax.fori_loop(0, count, body, 0)


def store_own(ref, x, a, value, level):
    lo, hi = max(a, Y0[level]), min(a + value.shape[1], Y0[level] + B[level])
    if lo < hi:
        ref[x, :, lo:hi, :] = value[:, lo - a : hi - a, :]


def restrict_rows(src, tmp, out, count, cy, first_plane, first_row, rows):
    size = min(4, count)

    def body(i, carry):
        for k in range(size):
            x = first_plane + 2 * (i * size + k)
            tmp[k] = 0.25 * (src[x, :, 0:rows, :] + src[x + 2, :, 0:rows, :]) + 0.5 * src[x + 1, :, 0:rows, :]
        for k in range(size):
            for z in range(src.shape[1]):
                v = 0.25 * (
                    tmp[k, z, pl.ds(first_row, cy, stride=2), :]
                    + tmp[k, z, pl.ds(first_row + 2, cy, stride=2), :]
                ) + 0.5 * tmp[k, z, pl.ds(first_row + 1, cy, stride=2), :]
                at = (i * size + k) * cy
                if cy % 8 == 0:
                    at = pl.multiple_of(at, 8)
                out[z, pl.ds(at, cy), :] = v
        return carry

    lax.fori_loop(0, count // size, body, 0)


def split_restrict(level, src, tmp, mid, matrix, target):
    cb = B[level + 1]
    x1, y1 = X0[level + 1], Y0[level + 1]
    restrict_rows(src, tmp, mid, cb, cb, X0[level], Y0[level], 8 * (CH[level] + 2))
    total = None
    for z in range(ZT[level]):
        part = dot(mid[z], matrix[z])
        total = part if total is None else total + part
    for i in range(cb):
        for z in range(ZT[level + 1]):
            target[x1 + i, z, y1 : y1 + cb, :] = total[i * cb : (i + 1) * cb, 128 * z : 128 * z + 128]


def interleave(ez, target, count, t0, rows, nj, first_plane, first_row):
    for_z = range(target.shape[1])

    def body(i, carry):
        t = t0 + i
        for z in for_z:
            a1, b1 = ez[t, z, rows : rows + nj, :], ez[t, z, rows - 1 : rows - 1 + nj, :]
            a0, b0 = ez[t - 1, z, rows : rows + nj, :], ez[t - 1, z, rows - 1 : rows - 1 + nj, :]
            odd, even = a1, 0.5 * (a1 + b1)
            odd_0, even_0 = a0, 0.5 * (a0 + b0)
            x = first_plane + 2 * i
            target[x, z, pl.ds(first_row + 1, nj, stride=2), :] = 0.5 * (odd_0 + odd)
            target[x, z, pl.ds(first_row, nj, stride=2), :] = 0.5 * (even_0 + even)
            target[x + 1, z, pl.ds(first_row + 1, nj, stride=2), :] = odd
            target[x + 1, z, pl.ds(first_row, nj, stride=2), :] = even
        return carry

    lax.fori_loop(0, count, body, 0)


def kernel(f_hbm, s_hbm, out_hbm, *refs):
    it = iter(refs)
    lev = []
    for l in range(3):
        me = dict(ch=CH[l], xsum=x_plain, zsum=z_split, tall=(8, 32, 24)[l], width=128)
        for name in ("r", "s", "rho", "tmp", "mid"):
            me[name] = next(it)
        if l == 0:
            me["d"] = [next(it) for _ in range(4)]
            me["gi"], me["f"] = next(it), next(it)
            me["x"] = me["d"][0]
            me["ez"] = me["r"].at[pl.ds(0, 21), :, pl.ds(0, 24), :]
        else:
            old = lev[0]["d"]
            if l == 1:
                views = [old[n].at[pl.ds(0, 32), pl.ds(z, 2), pl.ds(0, 48), :] for n in (2, 3) for z in (0, 2)]
                me["gi"] = old[1].at[pl.ds(0, 32), pl.ds(0, 2), pl.ds(0, 48), :]
            else:
                views = [lev[0]["f"].at[pl.ds(0, 24), pl.ds(z, 1), pl.ds(0, 40), :] for z in range(4)]
                me["gi"] = old[1].at[pl.ds(0, 24), pl.ds(2, 1), pl.ds(0, 40), :]
            me["d"], me["f"] = views, me["r"]
            me["x"], me["ez"] = next(it), next(it)
        lev.append(me)
    for l in range(3, 6):
        me = dict(ch=(8, 4, 2)[l - 3], tall=(32, 32, 16)[l - 3], width=64)
        me["xsum"], me["zsum"] = (x_pairs, z_split) if l == 3 else (x_plain, z_open)
        for name in ("tmp", "mid"):
            me[name] = next(it)
        old = lev[0]["s"]
        if l == 3:
            me["gi"], me["x"] = next(it), next(it)
        elif l == 4:
            me["gi"], me["x"] = [old.at[pl.ds(20, 18), pl.ds(z, 1), pl.ds(0, 48), :] for z in (0, 1)]
        else:
            me["gi"], me["x"], r5, s5 = [old.at[pl.ds(0, 10), pl.ds(z, 1), pl.ds(0, 32), :] for z in range(4)]
            f5 = old.at[pl.ds(10, 10), pl.ds(0, 1), pl.ds(0, 32), :]
        me["ez"] = lev[0]["d"][1].at[pl.ds(0, 16), pl.ds(3, 1), pl.ds(0, 48), :] if l == 3 else next(it)
        if l == 3:
            fields = [next(it) for _ in range(7)]
        elif l == 4:
            old = lev[0]["r"]
            fields = [old.at[pl.ds(x, 18), pl.ds(z, 1), pl.ds(0, 48), :] for x in (0, 18) for z in range(4)][:7]
        else:
            old = lev[0]["f"]
            fields = [old.at[pl.ds(24, 10), pl.ds(z, 1), pl.ds(0, 32), :] for z in range(4)]
            fields += [r5, s5, f5]
        me["d"] = fields[:4]
        me["r"], me["s"], me["f"] = fields[4:]
        lev.append(me)
    blk_f, blk_s = next(it), next(it)
    rz0, pz0, rz1, pz1, rz2, pz2, rz3, pz3, rz4, pz4 = [next(it) for _ in range(10)]
    load_sem, send, recv, wsend, wrecv, gsend, grecv = [next(it) for _ in range(7)]
    gx, gy = lax.axis_index("gx"), lax.axis_index("gy")
    l0, l3, l4, l5 = lev[0], lev[3], lev[4], lev[5]

    loads = []
    for n, (hbm, ref) in enumerate(((s_hbm, l0["s"]), (f_hbm, l0["f"]))):
        for z in range(4):
            c = pltpu.make_async_copy(
                hbm.at[:, :, pl.ds(128 * z, 128)],
                ref.at[pl.ds(X0[0], 32), z, pl.ds(Y0[0], 32), :],
                load_sem.at[n, z],
            )
            c.start()
            loads.append(c)

    def clear_around(ref, off, top):
        n, _, rows, _ = ref.shape
        ref[0:off] = jnp.zeros((off, 1, rows, 128), F32)
        ref[n - off : n] = jnp.zeros((off, 1, rows, 128), F32)
        ref[:, :, 0:8, :] = jnp.zeros((n, 1, 8, 128), F32)
        ref[:, :, top:rows, :] = jnp.zeros((n, 1, rows - top, 128), F32)

    def clear_pads(l):
        me = lev[l]
        top = 8 + 8 * me["ch"]
        for ref in me["d"] + [me["s"]]:
            clear_around(ref, 1, top)
        clear_around(me["x"], 3 if l == 3 else 1, top)
        if l > 3:
            me["ez"][...] = jnp.zeros(me["ez"].shape, F32)
        me["mid"][...] = jnp.zeros(me["mid"].shape, F32)

    clear_pads(3)

    barrier = pltpu.get_barrier_semaphore()
    peers = list(DIRS) + [(d, 0) for d in range(2, GX - 1)] + [(0, d) for d in range(2, GY - 1)]
    for dx, dy in peers:
        pl.semaphore_signal(barrier, inc=1, device_id=device(dx, dy), device_id_type=MESH)
    pl.semaphore_wait(barrier, len(peers))

    slot = iter(range(16))
    rest = []

    def exchange(ref, l, depth, dirs=DIRS):
        return Exchange(ref, l, depth, send, recv, next(slot), dirs).start()

    def piece(c):
        lo, up = EDGE
        x = pl.ds(X0[0] + 8 * c, 8)
        out = []
        for n, ref in enumerate((l0["s"], l0["f"])):
            for m, dy in enumerate((-1, 1)):
                (sy, ny), (ty, _) = spans(dy, 32, lo, up, Y0[0])
                out.append(
                    remote(ref.at[x, :, pl.ds(sy, ny), :], ref.at[x, :, pl.ds(ty, ny), :],
                           wsend.at[c, 2 * n + m], wrecv.at[c, 2 * n + m], (0, dy))
                )
        return out

    for c in loads:
        c.wait()
    for c in piece(0):
        c.start()
    x_dirs = [d for d in DIRS if d[0]]
    ex_x = [exchange(l0["s"], 0, EDGE, x_dirs), exchange(l0["f"], 0, EDGE, x_dirs)]
    for n in range(1, 4):
        for c in piece(n):
            c.start()

    def fill(ref, index, fn):
        shape = ref.shape[1:]
        ref[index] = fn(lax.broadcasted_iota(jnp.int32, shape, 0), lax.broadcasted_iota(jnp.int32, shape, 1))

    def wr(z, k):
        return jnp.where(z == 2 * k + 1, 2.0, jnp.where((z == 2 * k) | (z == 2 * k + 2), 1.0, 0.0))

    def wp(k, z):
        return jnp.where(z == 2 * k + 1, 1.0, jnp.where((z == 2 * k) | (z == 2 * k + 2), 0.5, 0.0))

    for t in range(4):
        fill(rz0, t, lambda z, k: wr(z + 128 * t, k))
    for t in range(2):
        fill(pz0, t, lambda k, z: wp(k + 128 * t, z))
        fill(rz1, t, lambda z, k: wr(z + 128 * t, k))
    fill(pz1, 0, wp)
    for h in range(2):
        fill(rz2, h, lambda z, k: jnp.where((k >> 6) == h, wr(z, k & 63), 0.0))
        fill(pz2, h, lambda k, z: jnp.where((k >> 6) == h, wp(k & 63, z), 0.0))
    fill(rz3, 0, lambda z, k: jnp.where(k < 32, wr(z & 63, k) * jnp.where(z < 64, 0.25, 0.5), 0.0))
    fill(rz3, 1, lambda z, k: jnp.where((k < 32) & (z < 64), wr(z, k) * 0.25, 0.0))
    fill(pz3, 0, lambda k, z: jnp.where(k < 32, wp(k, z & 63) * jnp.where(z < 64, 0.5, 1.0), 0.0))
    fill(pz3, 1, lambda k, z: jnp.where((k < 32) & (z < 64), wp(k, z) * 0.5, 0.0))
    fill(rz4, 0, lambda z, k: jnp.where((k < 16) & (z < 32), wr(z, k), 0.0))
    fill(pz4, 0, lambda k, z: jnp.where((k < 16) & (z < 32), wp(k, z), 0.0))
    rz, pz = (rz0, rz1), (pz0, pz1)

    def pack_block(src, blk):
        mid = lev[2]["mid"]
        restrict_rows(src, lev[2]["tmp"], mid, 4, 4, X0[2], Y0[2], 40)
        lo, hi = dot(mid[0], rz2[0]), dot(mid[0], rz2[1])
        for i in range(2):
            blk[i, 0, 0:4, :] = lo[8 * i : 8 * i + 4] + hi[8 * i + 4 : 8 * i + 8]

    class Gather:
        def __init__(self, n, blk, ref):
            own = ref.at[pl.ds(1 + 2 * gx, 2), :, pl.ds(8 + 4 * gy, 4), :]
            src = blk.at[:, :, pl.ds(0, 4), :]
            slab = ref.at[pl.ds(1, 16), :, pl.ds(8 + 4 * gy, 4), :]
            self.local = pltpu.make_async_copy(src, own, load_sem.at[2, n])
            self.first = [remote(src, own, gsend.at[n, d], grecv.at[n, d], (d, 0)) for d in range(1, GX)]
            self.second = [
                remote(slab, slab, gsend.at[n, 8 + d], grecv.at[n, 8 + d], (0, d)) for d in range(1, GY)
            ]

        def start(self):
            for c in self.first:
                c.start()
            self.local.start()

        def middle(self):
            self.local.wait()
            for c in self.first:
                c.wait_recv()
            for c in self.second:
                c.start()

        def finish(self):
            for c in self.second:
                c.wait_recv()

        def wait_send(self):
            for c in self.first + self.second:
                c.wait_send()

    gather_s = Gather(0, blk_s, l3["s"])
    gather_f = Gather(1, blk_f, l3["f"])

    def edge_mask(l):
        row_lo = jnp.where(gy == 0, Y0[l], 0)
        row_hi = jnp.where(gy == GY - 1, Y0[l] + B[l], 1000)
        x_lo = jnp.where(gx == 0, X0[l], 0)
        x_hi = jnp.where(gx == GX - 1, X0[l] + B[l], 1000)

        def mask(v, x):
            row = lax.broadcasted_iota(jnp.int32, v.shape, 1) + 8
            inside = (row >= row_lo) & (row < row_hi) & (x >= x_lo) & (x < x_hi)
            return jnp.where(inside, v, 0.0)

        return mask

    def pre_stage(l, k, x_range):
        me, b = lev[l], B[l]
        d, r = me["d"], me["r"]
        lo, hi = x_range[0] + X0[l], x_range[1] + X0[l]
        if k < 3:
            smooth_step(me, d[k], r, (lo, hi), d[k + 1], *FACTORS[k], r_out=r)
            return

        def residual(x, a, _, new):
            s = slice(a, a + new.shape[1])
            r[x, :, s, :] = (26.0 + me["s"][x, :, s, :]) * new

        def extra(x, a, dd, new):
            residual(x, a, dd, new)
            store_own(me["rho"], x, a, new, l)
            s = slice(a, a + new.shape[1])
            total = ((d[0][x, :, s, :] + d[1][x, :, s, :]) + d[2][x, :, s, :]) + dd
            if l:
                store_own(me["x"], x, a, total, l)
            else:
                me["x"][x, :, s, :] = total

        end = X0[l] + b
        inside = hi if x_range[1] <= b else end
        if inside > lo:
            smooth_step(me, d[3], r, (lo, inside), extra=extra)
        if inside < hi:
            smooth_step(me, d[3], r, (inside, hi), extra=residual)

    def pre(l):
        me, b = lev[l], B[l]
        begin(me, X0[l] - 7, b + 13, me["ch"], edge_mask(l))
        for k in range(4):
            pre_stage(l, k, (min(k - 3, 0), b + 4 - k))

    def post(l, emit, after=None):
        me, b = lev[l], B[l]
        dl = me["d"][1:] + [me["r"]]
        rho = me["rho"]
        lo, up = OUTER[l]

        def span(w):
            return X0[l] - lo - w, X0[l] + b + up + w

        smooth_step(me, dl[0], rho, span(3), dl[1], 0.0, 1.0 / CENTER, r_out=rho)
        smooth_step(me, dl[1], rho, span(2), dl[2], *FACTORS[0], r_out=rho)
        smooth_step(me, dl[2], rho, span(1), dl[3], *FACTORS[1], r_out=rho)
        al, be = FACTORS[2]

        def extra(x, a, dd, new):
            s = slice(a, a + new.shape[1])
            total = (me["x"][x, :, s, :] + dl[0][x, :, s, :]) + (dl[1][x, :, s, :] + dl[2][x, :, s, :])
            emit(x, a, (total + dd) + (al * dd + be * new))

        smooth_step(me, dl[3], rho, span(0), extra=extra, after=after)

    mask0 = edge_mask(0)

    def wave(x, count):
        begin(l0, X0[0] + x, count, 6, mask0)

    for c in piece(0):
        c.wait_recv()
    wave(0, 8)
    for k in range(3):
        pre_stage(0, k, (k + 1, 7 - k))

    def wave_body(n, carry):
        for c in piece(n):
            c.wait_recv()
        x = 8 * n
        wave(x, 8)
        for k in range(4):
            pre_stage_at(k, x - 1 - k)
        return carry

    def pre_stage_at(k, x):
        d, r = l0["d"], l0["r"]
        lo = X0[0] + x
        if k < 3:
            smooth_step(l0, d[k], r, (lo, lo + 8), d[k + 1], *FACTORS[k], r_out=r, count=8)
        else:
            smooth_step(l0, d[3], r, (lo, lo + 8), extra=last_pre, count=8)

    def last_pre(x, a, dd, new):
        d, s = l0["d"], slice(a, a + new.shape[1])
        l0["r"][x, :, s, :] = (26.0 + l0["s"][x, :, s, :]) * new
        store_own(l0["rho"], x, a, new, 0)
        d[0][x, :, s, :] = ((d[0][x, :, s, :] + d[1][x, :, s, :]) + d[2][x, :, s, :]) + dd

    lax.fori_loop(1, 4, wave_body, 0)
    for ex in ex_x:
        ex.wait_recv()
    wave(32, 5)
    for k in range(4):
        pre_stage(0, k, (31 - k, 36 - k))
    wave(-4, 4)
    for k in range(4):
        pre_stage(0, k, (k - 3, k + 1))

    zero_outside(l0["s"], 0)
    split_restrict(0, l0["s"], l0["tmp"], l0["mid"], rz[0], lev[1]["s"])
    ex_s = exchange(lev[1]["s"], 1, (6, 5))
    rest.append(ex_s)
    split_restrict(0, l0["r"], l0["tmp"], l0["mid"], rz[0], lev[1]["r"])
    ex_f = exchange(lev[1]["r"], 1, EDGE)
    ex_rho = [exchange(l0["rho"], 0, (3, 3))]
    ex_iter = [None]
    for ex in ex_x:
        ex.wait_send()
    for n in range(4):
        for c in piece(n):
            c.wait_send()
    clear_pads(4)
    clear_pads(5)
    l3["ez"][:, :, 0:8, :] = jnp.zeros((16, 1, 8, 128), F32)

    ex_s.wait_recv()
    zero_outside(lev[1]["s"], 1)
    split_restrict(1, lev[1]["s"], lev[1]["tmp"], lev[1]["mid"], rz[1], lev[2]["s"])
    ex_s = exchange(lev[2]["s"], 2, (7, 6))
    rest.append(ex_s)
    ex_f.wait_recv()
    ex_f.wait_send()
    pre(1)
    split_restrict(1, lev[1]["r"], lev[1]["tmp"], lev[1]["mid"], rz[1], lev[2]["r"])
    ex_f = exchange(lev[2]["r"], 2, EDGE)
    ex_rho.append(exchange(lev[1]["rho"], 1, (6, 5)))
    ex_iter.append(exchange(lev[1]["x"], 1, (3, 2)))
    ex_s.wait_recv()
    zero_outside(lev[2]["s"], 2)
    pack_block(lev[2]["s"], blk_s)
    gather_s.start()
    ex_f.wait_recv()
    ex_f.wait_send()
    pre(2)
    pack_block(lev[2]["r"], blk_f)
    gather_f.start()
    gather_s.middle()
    ex_rho.append(exchange(lev[2]["rho"], 2, (7, 6)))
    ex_iter.append(exchange(lev[2]["x"], 2, (4, 3)))
    gather_f.middle()
    rest += [gather_s, gather_f]

    def down_pairs(src, target):
        mid = l3["mid"]

        def body(i, carry):
            v = 0.25 * (src[1 + i, 0, pl.ds(8, 32, stride=2), :] + src[1 + i, 0, pl.ds(10, 32, stride=2), :])
            mid[0, pl.ds(pl.multiple_of(32 * i, 8), 32), :] = v + 0.5 * src[1 + i, 0, pl.ds(9, 32, stride=2), :]
            return carry

        lax.fori_loop(0, 16, body, 0)
        total = dot(mid[0, 0:512, :], rz3[0]) + dot(mid[0, 32:544, :], rz3[1])
        for i in range(16):
            target[1 + i, 0, 8:40, :] = total[32 * i : 32 * i + 32]

    def down_whole(src, target):
        mid = l4["mid"]
        restrict_rows(src, l4["tmp"], mid, 8, 16, 1, 8, 48)
        total = dot(mid[0], rz4[0])
        for i in range(8):
            target[1 + i, 0, 8:24, :] = total[16 * i : 16 * i + 16]

    gather_s.finish()
    down_pairs(l3["s"], l4["s"])
    down_whole(l4["s"], l5["s"])
    gather_f.finish()

    def whole_pre(l, planes):
        me = lev[l]
        d, r = me["d"], me["r"]
        lanes = (128, 32, 16)[l - 3]

        def mask(v, x):
            return v if lanes == 128 else jnp.where(lanes_of(v.shape) < lanes, v, 0.0)

        begin(me, 1, planes, me["ch"], mask)
        for k in range(3):
            smooth_step(me, d[k], r, (1, 1 + planes), d[k + 1], *FACTORS[k], r_out=r)

    def whole_residual(l, planes, f):
        me = lev[l]
        d, r = me["d"], me["r"]
        more = 2 if l == 3 else 0

        def extra(x, a, dd, new):
            s = slice(a, a + new.shape[1])
            me["x"][x + more, :, s, :] = ((d[0][x, :, s, :] + d[1][x, :, s, :]) + d[2][x, :, s, :]) + dd
            f[x, :, s, :] = (26.0 + me["s"][x, :, s, :]) * new

        smooth_step(me, d[3], r, (1, 1 + planes), r_out=r, extra=extra)

    def whole_post(l, planes):
        me = lev[l]
        d, r = me["d"], me["r"]
        span = (1, 1 + planes)
        more = 2 if l == 3 else 0
        smooth_step(me, d[0], r, span, d[1], 0.0, 1.0 / CENTER, r_out=r)
        smooth_step(me, d[1], r, span, d[2], *FACTORS[0], r_out=r)
        smooth_step(me, d[2], r, span, d[3], *FACTORS[1], r_out=r)
        al, be = FACTORS[2]

        def extra(x, a, dd, new):
            s = slice(a, a + new.shape[1])
            total = (me["x"][x + more, :, s, :] + d[0][x, :, s, :]) + (d[1][x, :, s, :] + d[2][x, :, s, :])
            me["x"][x + more, :, s, :] = (total + dd) + (al * dd + be * new)

        smooth_step(me, d[3], r, span, extra=extra)

    whole_pre(3, 16)
    whole_residual(3, 16, l3["d"][0])
    down_pairs(l3["d"][0], l4["f"])
    whole_pre(4, 16)
    whole_residual(4, 16, l4["d"][0])
    down_whole(l4["d"][0], l5["f"])

    whole_pre(5, 8)
    d5, r5 = l5["d"], l5["r"]

    def turn(x, a, dd, new):
        s = slice(a, a + new.shape[1])
        l5["x"][x, :, s, :] = ((d5[0][x, :, s, :] + d5[1][x, :, s, :]) + d5[2][x, :, s, :]) + dd

    smooth_step(l5, d5[3], r5, (1, 9), d5[0], 0.0, 1.0 / CENTER, r_out=r5, extra=turn)
    for k in range(2):
        smooth_step(l5, d5[k], r5, (1, 9), d5[k + 1], *FACTORS[k], r_out=r5)
    al, be = FACTORS[2]

    def last(x, a, dd, new):
        s = slice(a, a + new.shape[1])
        total = (l5["x"][x, :, s, :] + d5[0][x, :, s, :]) + d5[1][x, :, s, :]
        l5["x"][x, :, s, :] = (total + dd) + (al * dd + be * new)

    smooth_step(l5, d5[2], r5, (1, 9), extra=last)

    up = dot(l5["x"][1:9, 0, 8:24, :].reshape(128, 128), pz4[0])
    for i in range(8):
        l4["ez"][1 + i, 0, 8:24, :] = up[16 * i : 16 * i + 16]
    interleave(l4["ez"], l4["d"][0], 8, 1, 8, 16, 1, 8)
    whole_post(4, 16)

    e4 = l4["x"]
    up = dot(e4[1:17, 0, 8:40, :].reshape(512, 128), pz3[0]) + dot(e4[0:16, 0, 8:40, :].reshape(512, 128), pz3[1])
    for i in range(16):
        l3["ez"][i, 0, 8:40, :] = up[32 * i : 32 * i + 32]

    def rows_up(i, carry):
        a, b = l3["ez"][i, 0, 8:40, :], l3["ez"][i, 0, 7:39, :]
        l3["d"][0][1 + i, 0, pl.ds(9, 32, stride=2), :] = a
        l3["d"][0][1 + i, 0, pl.ds(8, 32, stride=2), :] = 0.5 * (a + b)
        return carry

    lax.fori_loop(0, 16, rows_up, 0)
    whole_post(3, 16)

    def correct(l, t0, row, nj):
        count = (20, 15, 12)[l]
        interleave(lev[l]["ez"], lev[l]["d"][1], count, t0, row, nj, 0, 8)
        zero_outside(lev[l]["d"][1], l, lower=False)
        ex_rho[l].wait_recv()
        ex_rho[l].wait_send()
        zero_outside(lev[l]["rho"], l)
        if l:
            ex_iter[l].wait_recv()
            ex_iter[l].wait_send()
            zero_outside(lev[l]["x"], l)

    def emit_to(l):
        def emit(x, a, v):
            lev[l]["x"][x, :, a : a + v.shape[1], :] = v
        return emit

    win = l3["x"][pl.ds(2 * gx, 7), 0, pl.ds(4 * gy, 24), :].reshape(168, 128)
    for h in range(2):
        up = dot(win, pz2[h])
        for m in range(7):
            lev[2]["ez"][2 * m + h, 0] = up[24 * m : 24 * m + 24]
    correct(2, 2, 4, 16)
    post(2, emit_to(2))

    def lift(l, first_plane, first_row, planes, rows, step):
        e, ez = lev[l + 1]["x"], lev[l]["ez"]
        for t in range(0, planes, step):
            total = None
            for z in range(ZT[l + 1]):
                v = e[first_plane + t : first_plane + t + step, z, first_row : first_row + rows, :]
                part = dot(v.reshape(step * rows, 128), pz[l][z])
                total = part if total is None else total + part
            for k in range(step):
                for z in range(ZT[l]):
                    ez[t + k, z] = total[rows * k : rows * k + rows, 128 * z : 128 * z + 128]

    lift(1, 3, 8, 16, 24, 16)
    correct(1, 1, 4, 16)
    post(1, emit_to(1))
    lift(0, 5, 13, 21, 24, 7)
    correct(0, 1, 1, 20)

    def store(i, x):
        return [
            pltpu.make_async_copy(
                l0["x"].at[pl.ds(x, 8), z, pl.ds(Y0[0], 32), :],
                out_hbm.at[pl.ds(x - X0[0], 8), :, pl.ds(128 * z, 128)],
                load_sem.at[4 + i, z],
            )
            for z in range(4)
        ]

    def after(i, x):
        for c in store(i, x):
            c.start()

    post(0, emit_to(0), after)
    for ex in rest:
        ex.wait_send()
    for i in range(4):
        for c in store(i, X0[0] + 8 * i):
            c.wait()


def per_device(right_side, absorption):
    scratch = []

    def vmem(*shape):
        scratch.append(pltpu.VMEM(shape, F32))

    for l in range(3):
        planes, zt, rows = PLANES[l], ZT[l], ROWS[l]
        for _ in range(3):
            vmem(planes, zt, rows, 128)
        vmem(8, zt, 8 * (CH[l] + 2), 128)
        vmem(zt, (256, 64, 16)[l], 128)
        if l == 0:
            for _ in range(6):
                vmem(planes, zt, rows, 128)
        else:
            vmem(planes, zt, rows, 128)
            vmem(*((16, 2, 24, 128), (14, 1, 24, 128))[l - 1])
    for l in range(3, 6):
        vmem(8, 1, (80, 48, 32)[l - 3], 128)
        vmem(1, (544, 128, 8)[l - 3], 128)
        if l == 3:
            vmem(18, 1, 80, 128)
            vmem(22, 1, 88, 128)
            for _ in range(7):
                vmem(18, 1, 80, 128)
        else:
            vmem(*((9, 1, 32, 128), (1, 1, 8, 128))[l - 4])
    vmem(2, 1, 8, 128)
    vmem(2, 1, 8, 128)
    for shape in ((4, 128, 256), (2, 128, 512), (2, 128, 128), (1, 128, 256), (2, 128, 128), (2, 128, 128),
                  (2, 128, 128), (2, 128, 128), (1, 128, 128), (1, 128, 128)):
        vmem(*shape)
    dma = pltpu.SemaphoreType.DMA
    scratch += [dma((8, 4)), dma((12, 8)), dma((12, 8)), dma((4, 4)), dma((4, 4)), dma((2, 24)), dma((2, 24))]
    return pl.pallas_call(
        kernel,
        out_shape=jax.ShapeDtypeStruct((32, 32, 512), F32),
        in_specs=[pl.BlockSpec(memory_space=pl.ANY)] * 2,
        out_specs=pl.BlockSpec(memory_space=pl.ANY),
        scratch_shapes=scratch,
        compiler_params=pltpu.CompilerParams(
            collective_id=0, has_side_effects=True, vmem_limit_bytes=63 * 2**20
        ),
        name="vcycle",
    )(right_side, absorption)


def solution(mesh):
    spec = P("gx", "gy", None)
    return jax.shard_map(per_device, mesh=mesh, in_specs=(spec, spec), out_specs=spec, check_vma=False)
```

time: 124 us -> 108 us (0.87)
  Pallas kernels: 120 us -> 105 us
    pallas_call x1, Pallas kernels: 120 us -> 105 us  [per_device(): pl.pallas_call(kernel, out_shape=jax.ShapeDtypeStruct((32, 32, 512), F32)...]
where the time goes in v2:
time: 108 us
  Pallas kernels  105 us (97%)
  local copies, waits for them, and re-layouts  3.19 us (3%)
    pallas_call x1, Pallas kernels, per_device(): pl.pallas_call(kernel, out_shape=jax.ShapeDtypeStruct((32, 32, 512), F32)...  105 us
    unnamed x1, local copies, waits for them, and re-layouts  3.19 us

profile of v2, /device:TPU:1, one launch (start us, length us, event | category | flops | bytes accessed | tf_op | source)
XLA Modules:
  0.0 107.9 jit_solution(1968021838614017175)
XLA Ops:
  0.0 104.7 %vcycle.1 = f32[32,32,512]{2,1,0:T(8,128)} custom-call(f32[32,32,512]{2,1,0:T(8,128)} %f_hbm.1, f32[32,32,512]{2,1,0:T(8,128)} %s_hbm.1), custom_call_target="tpu_custom_call" | custom-call | tf_op jit(solution)/shard_map/vcycle/pallas_call | solution.py:824
  104.7 3.2 %copy.4 = f32[32,32,512]{2,1,0:T(8,128)} copy(f32[32,32,512]{2,1,0:T(8,128)} %vcycle.1) | data formatting | bytes 4194304

commit v3 on v2

--- a/solution.py
+++ b/solution.py
@@ -41,7 +41,17 @@
 
 
 def dot(a, b):
-    return jnp.dot(a, b, precision=lax.Precision.HIGHEST, preferred_element_type=F32)
+    total = None
+    for part in range(3):
+        if part < 2:
+            t = a * 65537.0
+            top = t - (t - a)
+        else:
+            top = a
+        p = jnp.dot(top, b, preferred_element_type=F32)
+        total = p if total is None else total + p
+        a = a - top
+    return total
 
 
 def spans(way, width, lo, up, start):
@@ -213,28 +223,37 @@
     size = min(4, count)
 
     def body(i, carry):
-        for k in range(size):
-            x = first_plane + 2 * (i * size + k)
-            tmp[k] = 0.25 * (src[x, :, 0:rows, :] + src[x + 2, :, 0:rows, :]) + 0.5 * src[x + 1, :, 0:rows, :]
-        for k in range(size):
-            for z in range(src.shape[1]):
-                v = 0.25 * (
-                    tmp[k, z, pl.ds(first_row, cy, stride=2), :]
-                    + tmp[k, z, pl.ds(first_row + 2, cy, stride=2), :]
-                ) + 0.5 * tmp[k, z, pl.ds(first_row + 1, cy, stride=2), :]
-                at = (i * size + k) * cy
-                if cy % 8 == 0:
-                    at = pl.multiple_of(at, 8)
-                out[z, pl.ds(at, cy), :] = v
+        restrict_group(i, size, src, tmp, out, cy, first_plane, first_row, rows)
         return carry
 
     lax.fori_loop(0, count // size, body, 0)
+
+
+def restrict_group(i, size, src, tmp, out, cy, first_plane, first_row, rows):
+    for k in range(size):
+        x = first_plane + 2 * (i * size + k)
+        tmp[k] = 0.25 * (src[x, :, 0:rows, :] + src[x + 2, :, 0:rows, :]) + 0.5 * src[x + 1, :, 0:rows, :]
+    for k in range(size):
+        for z in range(src.shape[1]):
+            v = 0.25 * (
+                tmp[k, z, pl.ds(first_row, cy, stride=2), :]
+                + tmp[k, z, pl.ds(first_row + 2, cy, stride=2), :]
+            ) + 0.5 * tmp[k, z, pl.ds(first_row + 1, cy, stride=2), :]
+            at = (i * size + k) * cy
+            if cy % 8 == 0:
+                at = pl.multiple_of(at, 8)
+            out[z, pl.ds(at, cy), :] = v
 
 
 def split_restrict(level, src, tmp, mid, matrix, target):
     cb = B[level + 1]
+    restrict_rows(src, tmp, mid, cb, cb, X0[level], Y0[level], 8 * (CH[level] + 2))
+    split_finish(level, mid, matrix, target)
+
+
+def split_finish(level, mid, matrix, target):
+    cb = B[level + 1]
     x1, y1 = X0[level + 1], Y0[level + 1]
-    restrict_rows(src, tmp, mid, cb, cb, X0[level], Y0[level], 8 * (CH[level] + 2))
     total = None
     for z in range(ZT[level]):
         part = dot(mid[z], matrix[z])
@@ -274,7 +293,7 @@
         if l == 0:
             me["d"] = [next(it) for _ in range(4)]
             me["gi"], me["f"] = next(it), next(it)
-            me["x"] = me["d"][0]
+            me["x"] = me["f"]
             me["ez"] = me["r"].at[pl.ds(0, 21), :, pl.ds(0, 24), :]
         else:
             old = lev[0]["d"]
@@ -282,7 +301,7 @@
                 views = [old[n].at[pl.ds(0, 32), pl.ds(z, 2), pl.ds(0, 48), :] for n in (2, 3) for z in (0, 2)]
                 me["gi"] = old[1].at[pl.ds(0, 32), pl.ds(0, 2), pl.ds(0, 48), :]
             else:
-                views = [lev[0]["f"].at[pl.ds(0, 24), pl.ds(z, 1), pl.ds(0, 40), :] for z in range(4)]
+                views = [old[0].at[pl.ds(0, 24), pl.ds(z, 1), pl.ds(0, 40), :] for z in range(4)]
                 me["gi"] = old[1].at[pl.ds(0, 24), pl.ds(2, 1), pl.ds(0, 40), :]
             me["d"], me["f"] = views, me["r"]
             me["x"], me["ez"] = next(it), next(it)
@@ -307,7 +326,7 @@
             old = lev[0]["r"]
             fields = [old.at[pl.ds(x, 18), pl.ds(z, 1), pl.ds(0, 48), :] for x in (0, 18) for z in range(4)][:7]
         else:
-            old = lev[0]["f"]
+            old = lev[0]["d"][0]
             fields = [old.at[pl.ds(24, 10), pl.ds(z, 1), pl.ds(0, 32), :] for z in range(4)]
             fields += [r5, s5, f5]
         me["d"] = fields[:4]
@@ -315,7 +334,7 @@
         lev.append(me)
     blk_f, blk_s = next(it), next(it)
     rz0, pz0, rz1, pz1, rz2, pz2, rz3, pz3, rz4, pz4 = [next(it) for _ in range(10)]
-    load_sem, send, recv, wsend, wrecv, gsend, grecv = [next(it) for _ in range(7)]
+    load_sem, send, recv, wsend, wrecv, gsend, grecv, hello = [next(it) for _ in range(8)]
     gx, gy = lax.axis_index("gx"), lax.axis_index("gy")
     l0, l3, l4, l5 = lev[0], lev[3], lev[4], lev[5]
 
@@ -347,13 +366,20 @@
             me["ez"][...] = jnp.zeros(me["ez"].shape, F32)
         me["mid"][...] = jnp.zeros(me["mid"].shape, F32)
 
+    barrier = pltpu.get_barrier_semaphore()
+    for dx, dy in DIRS:
+        pl.semaphore_signal(barrier, inc=1, device_id=device(dx, dy), device_id_type=MESH)
     clear_pads(3)
-
-    barrier = pltpu.get_barrier_semaphore()
-    peers = list(DIRS) + [(d, 0) for d in range(2, GX - 1)] + [(0, d) for d in range(2, GY - 1)]
-    for dx, dy in peers:
-        pl.semaphore_signal(barrier, inc=1, device_id=device(dx, dy), device_id_type=MESH)
-    pl.semaphore_wait(barrier, len(peers))
+    pl.semaphore_wait(barrier, len(DIRS))
+
+    rounds = (((1, 0), (-1, 0), (0, 1), (0, -1)), ((2, 0), (-2, 0), (0, 2), (0, -2)), ((0, 4), (0, -4)))
+
+    def greet(n):
+        for dx, dy in rounds[n]:
+            pl.semaphore_signal(hello.at[n], inc=1, device_id=device(dx, dy), device_id_type=MESH)
+
+    def greeted(n):
+        pl.semaphore_wait(hello.at[n], len(rounds[n]))
 
     slot = iter(range(16))
     rest = []
@@ -362,10 +388,9 @@
         return Exchange(ref, l, depth, send, recv, next(slot), dirs).start()
 
     def piece(c):
-        lo, up = EDGE
         x = pl.ds(X0[0] + 8 * c, 8)
         out = []
-        for n, ref in enumerate((l0["s"], l0["f"])):
+        for n, (ref, (lo, up)) in enumerate(((l0["s"], (3, 4)), (l0["d"][0], EDGE))):
             for m, dy in enumerate((-1, 1)):
                 (sy, ny), (ty, _) = spans(dy, 32, lo, up, Y0[0])
                 out.append(
@@ -374,12 +399,29 @@
                 )
         return out
 
+    def begin_own(n, carry):
+        own = pl.ds(Y0[0], 32)
+
+        def body(i, inner):
+            x = X0[0] + 8 * n + i
+            g = 1.0 / (26.0 + l0["s"][x, :, own, :])
+            new = l0["f"][x, :, own, :] * g
+            l0["gi"][x, :, own, :] = g
+            l0["r"][x, :, own, :] = new
+            l0["d"][0][x, :, own, :] = new * (1.0 / CENTER)
+            return inner
+
+        return lax.fori_loop(0, 8, body, carry)
+
     for c in loads:
         c.wait()
+    begin_own(0, 0)
     for c in piece(0):
         c.start()
+    greet(0)
     x_dirs = [d for d in DIRS if d[0]]
-    ex_x = [exchange(l0["s"], 0, EDGE, x_dirs), exchange(l0["f"], 0, EDGE, x_dirs)]
+    lax.fori_loop(1, 4, begin_own, 0)
+    ex_x = [exchange(l0["s"], 0, (3, 4), x_dirs), exchange(l0["d"][0], 0, EDGE, x_dirs)]
     for n in range(1, 4):
         for c in piece(n):
             c.start()
@@ -458,8 +500,8 @@
         x_lo = jnp.where(gx == 0, X0[l], 0)
         x_hi = jnp.where(gx == GX - 1, X0[l] + B[l], 1000)
 
-        def mask(v, x):
-            row = lax.broadcasted_iota(jnp.int32, v.shape, 1) + 8
+        def mask(v, x, a=8):
+            row = lax.broadcasted_iota(jnp.int32, v.shape, 1) + a
             inside = (row >= row_lo) & (row < row_hi) & (x >= x_lo) & (x < x_hi)
             return jnp.where(inside, v, 0.0)
 
@@ -523,14 +565,33 @@
 
     mask0 = edge_mask(0)
 
-    def wave(x, count):
-        begin(l0, X0[0] + x, count, 6, mask0)
+    def wave(x, count, parts=((8, 4), (44, 5))):
+        @pl.when(gy == GY - 1)
+        def _():
+            l0["s"][pl.ds(X0[0] + x, count), :, 44:49, :] = jnp.zeros((count, 4, 5, 128), F32)
+
+        def body(i, carry):
+            at = X0[0] + x + i
+            for a, h in parts:
+                rows = slice(a, a + h)
+                l0["gi"][at, :, rows, :] = mask0(1.0 / (26.0 + l0["s"][at, :, rows, :]), at, a)
+                new = mask0(l0["d"][0][at, :, rows, :], at, a)
+                l0["d"][0][at, :, rows, :] = new
+                l0["r"][at, :, rows, :] = new * CENTER
+            return carry
+
+        lax.fori_loop(0, count, body, 0)
 
     for c in piece(0):
         c.wait_recv()
+    greeted(0)
+    greet(1)
     wave(0, 8)
     for k in range(3):
         pre_stage(0, k, (k + 1, 7 - k))
+
+    def lift_s(i):
+        restrict_group(i, 4, l0["s"], l0["tmp"], l0["mid"], 16, X0[0], Y0[0], 56)
 
     def wave_body(n, carry):
         for c in piece(n):
@@ -539,6 +600,7 @@
         wave(x, 8)
         for k in range(4):
             pre_stage_at(k, x - 1 - k)
+        lift_s(n - 1)
         return carry
 
     def pre_stage_at(k, x):
@@ -553,20 +615,27 @@
         d, s = l0["d"], slice(a, a + new.shape[1])
         l0["r"][x, :, s, :] = (26.0 + l0["s"][x, :, s, :]) * new
         store_own(l0["rho"], x, a, new, 0)
-        d[0][x, :, s, :] = ((d[0][x, :, s, :] + d[1][x, :, s, :]) + d[2][x, :, s, :]) + dd
-
-    lax.fori_loop(1, 4, wave_body, 0)
+        l0["x"][x, :, s, :] = ((d[0][x, :, s, :] + d[1][x, :, s, :]) + d[2][x, :, s, :]) + dd
+
+    lax.fori_loop(1, 3, wave_body, 0)
     for ex in ex_x:
         ex.wait_recv()
-    wave(32, 5)
+    greeted(1)
+    greet(2)
+    wave(-4, 4, ((8, 48),))
+    for k in range(4):
+        pre_stage(0, k, (k - 3, k + 1))
+    wave_body(3, 0)
+    wave(32, 5, ((8, 48),))
     for k in range(4):
         pre_stage(0, k, (31 - k, 36 - k))
-    wave(-4, 4)
-    for k in range(4):
-        pre_stage(0, k, (k - 3, k + 1))
-
-    zero_outside(l0["s"], 0)
-    split_restrict(0, l0["s"], l0["tmp"], l0["mid"], rz[0], lev[1]["s"])
+
+    @pl.when(gx == GX - 1)
+    def _():
+        l0["s"][X0[0] + 32] = jnp.zeros((4, 56, 128), F32)
+
+    lift_s(3)
+    split_finish(0, l0["mid"], rz[0], lev[1]["s"])
     ex_s = exchange(lev[1]["s"], 1, (6, 5))
     rest.append(ex_s)
     split_restrict(0, l0["r"], l0["tmp"], l0["mid"], rz[0], lev[1]["r"])
@@ -597,13 +666,14 @@
     ex_s.wait_recv()
     zero_outside(lev[2]["s"], 2)
     pack_block(lev[2]["s"], blk_s)
+    greeted(2)
     gather_s.start()
     ex_f.wait_recv()
     ex_f.wait_send()
+    gather_s.middle()
     pre(2)
     pack_block(lev[2]["r"], blk_f)
     gather_f.start()
-    gather_s.middle()
     ex_rho.append(exchange(lev[2]["rho"], 2, (7, 6)))
     ex_iter.append(exchange(lev[2]["x"], 2, (4, 3)))
     gather_f.middle()
@@ -784,6 +854,19 @@
     for i in range(4):
         for c in store(i, X0[0] + 8 * i):
             c.wait()
+
+
+def pass_on(src, dst, held, sem):
+    parts = [pl.ds(8 * n, 8) for n in range(4)]
+    into = [pltpu.make_async_copy(src.at[p], held.at[p], sem.at[0, n]) for n, p in enumerate(parts)]
+    out = [pltpu.make_async_copy(held.at[p], dst.at[p], sem.at[1, n]) for n, p in enumerate(parts)]
+    for c in into:
+        c.start()
+    for a, b in zip(into, out):
+        a.wait()
+        b.start()
+    for c in out:
+        c.wait()
 
 
 def per_device(right_side, absorption):
@@ -820,8 +903,8 @@
                   (2, 128, 128), (2, 128, 128), (1, 128, 128), (1, 128, 128)):
         vmem(*shape)
     dma = pltpu.SemaphoreType.DMA
-    scratch += [dma((8, 4)), dma((12, 8)), dma((12, 8)), dma((4, 4)), dma((4, 4)), dma((2, 24)), dma((2, 24))]
-    return pl.pallas_call(
+    scratch += [dma((8, 4)), dma((12, 8)), dma((12, 8)), dma((4, 4)), dma((4, 4)), dma((2, 24)), dma((2, 24)), pltpu.SemaphoreType.REGULAR((3,))]
+    result = pl.pallas_call(
         kernel,
         out_shape=jax.ShapeDtypeStruct((32, 32, 512), F32),
         in_specs=[pl.BlockSpec(memory_space=pl.ANY)] * 2,
@@ -832,6 +915,14 @@
         ),
         name="vcycle",
     )(right_side, absorption)
+    return pl.pallas_call(
+        pass_on,
+        out_shape=jax.ShapeDtypeStruct((32, 32, 512), F32),
+        in_specs=[pl.BlockSpec(memory_space=pl.ANY)],
+        out_specs=pl.BlockSpec(memory_space=pl.ANY),
+        scratch_shapes=[pltpu.VMEM((32, 32, 512), F32), dma((2, 4))],
+        name="pass_on",
+    )(result)
 
 
 def solution(mesh):

time: 108 us -> 100 us (0.926)
  Pallas kernels: 105 us -> 99.3 us
  local copies, waits for them, and re-layouts: 3.19 us -> 0 us
    pallas_call x1, Pallas kernels: 105 us -> 96.9 us  [per_device(): pl.pallas_call(kernel, out_shape=jax.ShapeDtypeStruct((32, 32, 512), F32)...]
    unnamed x1 -> x0, local copies, waits for them, and re-layouts: 3.19 us -> none
    pallas_call x0 -> x1, Pallas kernels: none -> 2.42 us  [per_device(): pl.pallas_call(pass_on, out_shape=jax.ShapeDtypeStruct((32, 32, 512), F32...]
where the time goes in v3:
time: 100 us; the launch traced here: 99.5 us
  Pallas kernels  99.3 us (99%)
    pallas_call x1, Pallas kernels, per_device(): pl.pallas_call(kernel, out_shape=jax.ShapeDtypeStruct((32, 32, 512), F32)...  96.9 us
    pallas_call x1, Pallas kernels, per_device(): pl.pallas_call(pass_on, out_shape=jax.ShapeDtypeStruct((32, 32, 512), F32...  2.42 us

profile of v3, /device:TPU:1, one launch (start us, length us, event | category | flops | bytes accessed | tf_op | source)
XLA Modules:
  0.0 99.5 jit_solution(10929340982824162804)
XLA Ops:
  0.0 96.9 %vcycle.1.src = f32[32,32,512]{2,1,0:T(8,128)} custom-call(f32[32,32,512]{2,1,0:T(8,128)} %f_hbm.1, f32[32,32,512]{2,1,0:T(8,128)} %s_hbm.1), custom_call_target="tpu_custom_call" | custom-call | tf_op jit(solution)/shard_map/vcycle/pallas_call | solution.py:907
  96.9 2.4 %pass_on.1 = f32[32,32,512]{2,1,0:T(8,128)} custom-call(f32[32,32,512]{2,1,0:T(8,128)} %vcycle.1.src), custom_call_target="tpu_custom_call" | custom-call | tf_op jit(solution)/shard_map/pass_on/pallas_call | solution.py:918

commit v4 on v3

--- a/solution.py
+++ b/solution.py
@@ -197,15 +197,25 @@
         group(first + full * size, rest)
 
 
-def begin(lev, first, count, chunks, mask):
-    gi, r, d, f, s = lev["gi"], lev["r"], lev["d"][0], lev["f"], lev["s"]
+def begin_gi(lev, first, count, chunks, mask):
+    gi, s = lev["gi"], lev["s"]
 
     def body(i, carry):
         x = first + i
         rows = slice(8, 8 + 8 * chunks)
-        g = mask(1.0 / (26.0 + s[x, :, rows, :]), x)
-        gi[x, :, rows, :] = g
-        new = f[x, :, rows, :] * g
+        gi[x, :, rows, :] = mask(1.0 / (26.0 + s[x, :, rows, :]), x)
+        return carry
+
+    lax.fori_loop(0, count, body, 0)
+
+
+def begin(lev, first, count, chunks):
+    gi, r, d, f = lev["gi"], lev["r"], lev["d"][0], lev["f"]
+
+    def body(i, carry):
+        x = first + i
+        rows = slice(8, 8 + 8 * chunks)
+        new = f[x, :, rows, :] * gi[x, :, rows, :]
         r[x, :, rows, :] = new
         d[x, :, rows, :] = new * (1.0 / CENTER)
         return carry
@@ -309,9 +319,14 @@
     for l in range(3, 6):
         me = dict(ch=(8, 4, 2)[l - 3], tall=(32, 32, 16)[l - 3], width=64)
         me["xsum"], me["zsum"] = (x_pairs, z_split) if l == 3 else (x_plain, z_open)
-        for name in ("tmp", "mid"):
-            me[name] = next(it)
         old = lev[0]["s"]
+        if l == 3:
+            me["tmp"] = next(it)
+        elif l == 4:
+            me["tmp"] = old.at[pl.ds(20, 16), pl.ds(2, 1), pl.ds(0, 48), :]
+        else:
+            me["tmp"] = old.at[pl.ds(10, 8), pl.ds(1, 1), pl.ds(0, 32), :]
+        me["mid"] = next(it)
         if l == 3:
             me["gi"], me["x"] = next(it), next(it)
         elif l == 4:
@@ -319,7 +334,10 @@
         else:
             me["gi"], me["x"], r5, s5 = [old.at[pl.ds(0, 10), pl.ds(z, 1), pl.ds(0, 32), :] for z in range(4)]
             f5 = old.at[pl.ds(10, 10), pl.ds(0, 1), pl.ds(0, 32), :]
-        me["ez"] = lev[0]["d"][1].at[pl.ds(0, 16), pl.ds(3, 1), pl.ds(0, 48), :] if l == 3 else next(it)
+        if l == 3:
+            me["ez"] = lev[0]["d"][1].at[pl.ds(0, 16), pl.ds(3, 1), pl.ds(0, 48), :]
+        else:
+            me["ez"] = old.at[pl.ds(10, 9), pl.ds(l - 2, 1), pl.ds(0, 32), :]
         if l == 3:
             fields = [next(it) for _ in range(7)]
         elif l == 4:
@@ -536,9 +554,12 @@
         if inside < hi:
             smooth_step(me, d[3], r, (inside, hi), extra=residual)
 
+    def pre_gi(l):
+        begin_gi(lev[l], X0[l] - 7, B[l] + 13, lev[l]["ch"], edge_mask(l))
+
     def pre(l):
         me, b = lev[l], B[l]
-        begin(me, X0[l] - 7, b + 13, me["ch"], edge_mask(l))
+        begin(me, X0[l] - 4, b + 9, me["ch"])
         for k in range(4):
             pre_stage(l, k, (min(k - 3, 0), b + 4 - k))
 
@@ -656,6 +677,7 @@
     split_restrict(1, lev[1]["s"], lev[1]["tmp"], lev[1]["mid"], rz[1], lev[2]["s"])
     ex_s = exchange(lev[2]["s"], 2, (7, 6))
     rest.append(ex_s)
+    pre_gi(1)
     ex_f.wait_recv()
     ex_f.wait_send()
     pre(1)
@@ -668,6 +690,7 @@
     pack_block(lev[2]["s"], blk_s)
     greeted(2)
     gather_s.start()
+    pre_gi(2)
     ex_f.wait_recv()
     ex_f.wait_send()
     gather_s.middle()
@@ -702,17 +725,18 @@
     gather_s.finish()
     down_pairs(l3["s"], l4["s"])
     down_whole(l4["s"], l5["s"])
+    for l, planes, lanes in ((3, 16, 128), (4, 16, 32), (5, 8, 16)):
+
+        def inside(v, x, lanes=lanes):
+            return jnp.where(lanes_of(v.shape) < lanes, v, 0.0)
+
+        begin_gi(lev[l], 1, planes, lev[l]["ch"], inside)
     gather_f.finish()
 
     def whole_pre(l, planes):
         me = lev[l]
         d, r = me["d"], me["r"]
-        lanes = (128, 32, 16)[l - 3]
-
-        def mask(v, x):
-            return v if lanes == 128 else jnp.where(lanes_of(v.shape) < lanes, v, 0.0)
-
-        begin(me, 1, planes, me["ch"], mask)
+        begin(me, 1, planes, me["ch"])
         for k in range(3):
             smooth_step(me, d[k], r, (1, 1 + planes), d[k + 1], *FACTORS[k], r_out=r)
 
@@ -888,15 +912,14 @@
             vmem(planes, zt, rows, 128)
             vmem(*((16, 2, 24, 128), (14, 1, 24, 128))[l - 1])
     for l in range(3, 6):
-        vmem(8, 1, (80, 48, 32)[l - 3], 128)
+        if l == 3:
+            vmem(16, 1, 80, 128)
         vmem(1, (544, 128, 8)[l - 3], 128)
         if l == 3:
             vmem(18, 1, 80, 128)
             vmem(22, 1, 88, 128)
             for _ in range(7):
                 vmem(18, 1, 80, 128)
-        else:
-            vmem(*((9, 1, 32, 128), (1, 1, 8, 128))[l - 4])
     vmem(2, 1, 8, 128)
     vmem(2, 1, 8, 128)
     for shape in ((4, 128, 256), (2, 128, 512), (2, 128, 128), (1, 128, 256), (2, 128, 128), (2, 128, 128),

time: 100 us -> 97.8 us (0.978)
  Pallas kernels: 99.3 us -> 96.9 us
    pallas_call x1, Pallas kernels: 96.9 us -> 94.5 us  [per_device(): pl.pallas_call(kernel, out_shape=jax.ShapeDtypeStruct((32, 32, 512), F32)...]
where the time goes in v4:
time: 97.8 us; the launch traced here: 97.1 us
  Pallas kernels  96.9 us (99%)
    pallas_call x1, Pallas kernels, per_device(): pl.pallas_call(kernel, out_shape=jax.ShapeDtypeStruct((32, 32, 512), F32)...  94.5 us
    pallas_call x1, Pallas kernels, per_device(): pl.pallas_call(pass_on, out_shape=jax.ShapeDtypeStruct((32, 32, 512), F32...  2.42 us

profile of v4, /device:TPU:1, one launch (start us, length us, event | category | flops | bytes accessed | tf_op | source)
XLA Modules:
  0.0 97.1 jit_solution(6113373501549761986)
XLA Ops:
  0.0 94.5 %vcycle.1.src = f32[32,32,512]{2,1,0:T(8,128)} custom-call(f32[32,32,512]{2,1,0:T(8,128)} %f_hbm.1, f32[32,32,512]{2,1,0:T(8,128)} %s_hbm.1), custom_call_target="tpu_custom_call" | custom-call | tf_op jit(solution)/shard_map/vcycle/pallas_call | solution.py:930
  94.5 2.4 %pass_on.1 = f32[32,32,512]{2,1,0:T(8,128)} custom-call(f32[32,32,512]{2,1,0:T(8,128)} %vcycle.1.src), custom_call_target="tpu_custom_call" | custom-call | tf_op jit(solution)/shard_map/pass_on/pallas_call | solution.py:941
